TPU v7x, 512 devices: a whole 4x4x16 slice. The times are simulated.
512 devices in a mesh: seq: 64 (over z, y), chan: 8 (over x, core).
Axes of the slice: x: 4, y: 4, z: 16, core: 2. Of those that a mesh axis runs over, the one named last changes fastest.
Arguments:
- values: bfloat16 [4096, 8192], P('seq', 'chan'), may hold values from -6 to 6
- gate: bfloat16 [4096, 8192], P('seq', 'chan'), may hold values from -6 to 6
- spectrum: float32 [8192, 2, 8192], P(('chan', 'seq')), may hold values from -6 to 6
- bias: float32 [8192], P('chan'), may hold values from -4 to 4
- out_weight: bfloat16 [8192, 8192], P('chan', 'seq'), may hold values from -0.1875 to 0.1875
Outputs:
- mixed: bfloat16 [4096, 8192], P('seq', 'chan')
All inputs are finite; a program needn't handle non-finite values.
Results may differ from a plain program's by a relative error of at most 0.017.
Values may be sent and summed in bfloat16 or wider, within the bound.
No kernel may reach another device: no remote copies, remote signals or barrier semaphores. Data moves between devices by JAX's collectives and lax.ppermute only.
A program may use at most 64 MiB of HBM per device.

v0:
```python
import math

import jax
import jax.numpy as jnp
from jax import lax
from jax.sharding import PartitionSpec as P

high = lax.Precision.HIGHEST


def tables(rows, cols, modulus):
    left = lax.broadcasted_iota(jnp.int32, (rows, cols), 0)
    right = lax.broadcasted_iota(jnp.int32, (rows, cols), 1)
    angle = 2.0 * math.pi / modulus * (left * right % modulus).astype(jnp.float32)
    return (jnp.cos(angle), jnp.sin(angle))


def mult(form, left, right):
    return jnp.einsum(form, left, right, precision=high)


def local_conv(signal, filt, block):
    width, length = signal.shape
    parts = length // block
    outer = 2 * parts
    total = 2 * length
    data = signal.astype(jnp.float32).reshape(width, parts, block)
    cos_one, sin_one = tables(outer, parts, outer)
    first_re = mult("kn,cnm->ckm", cos_one, data)
    first_im = -mult("kn,cnm->ckm", sin_one, data)
    tw_cos, tw_sin = tables(outer, block, total)
    turn_re = first_re * tw_cos + first_im * tw_sin
    turn_im = first_im * tw_cos - first_re * tw_sin
    cos_two, sin_two = tables(block, block, block)
    freq_re = mult("ckm,mq->cqk", turn_re, cos_two) + mult("ckm,mq->cqk", turn_im, sin_two)
    freq_im = mult("ckm,mq->cqk", turn_im, cos_two) - mult("ckm,mq->cqk", turn_re, sin_two)
    shaped = filt.reshape(width, 2, block, outer)
    filt_re = shaped[:, 0]
    filt_im = shaped[:, 1]
    prod_re = freq_re * filt_re - freq_im * filt_im
    prod_im = freq_re * filt_im + freq_im * filt_re
    back_re = mult("cqk,qm->cmk", prod_re, cos_two) - mult("cqk,qm->cmk", prod_im, sin_two)
    back_im = mult("cqk,qm->cmk", prod_re, sin_two) + mult("cqk,qm->cmk", prod_im, cos_two)
    inv_cos = tw_cos.T
    inv_sin = tw_sin.T
    spun_re = back_re * inv_cos - back_im * inv_sin
    spun_im = back_re * inv_sin + back_im * inv_cos
    cos_four, sin_four = tables(outer, parts, outer)
    result = mult("cmk,kt->ctm", spun_re, cos_four) - mult("cmk,kt->ctm", spun_im, sin_four)
    return (result * (1.0 / total)).reshape(width, length)


def per_device(values, gate, spectrum, bias, out_weight):
    rows, group = values.shape
    values_t = values.T
    moved_values = lax.all_to_all(values_t, "seq", split_axis=0, concat_axis=1, tiled=True)
    conv = local_conv(moved_values, spectrum, rows).astype(jnp.bfloat16)
    conv_back = lax.all_to_all(conv, "seq", split_axis=1, concat_axis=0, tiled=True).T
    gated = (
        gate.astype(jnp.float32)
        * (conv_back.astype(jnp.float32) + bias[None, :] * values.astype(jnp.float32))
    ).astype(jnp.bfloat16)
    partial_terms = jnp.dot(
        gated,
        lax.all_gather(out_weight, "seq", axis=1, tiled=True),
        preferred_element_type=jnp.float32,
    )
    return lax.psum_scatter(
        partial_terms.astype(jnp.bfloat16), "chan", scatter_dimension=1, tiled=True
    )


def solution(mesh):
    placed = (
        P("seq", "chan"),
        P("seq", "chan"),
        P(("chan", "seq"), None, None),
        P("chan"),
        P("chan", "seq"),
    )
    return jax.shard_map(
        per_device, mesh=mesh, in_specs=placed, out_specs=P("seq", "chan"), check_vma=False
    )
```

profile of v0, /device:TPU:1, one launch (start us, length us, event | category | flops | bytes accessed | tf_op | source)
XLA Modules:
  0.0 285.9 jit_solution(16255093739787348063)
XLA Ops:
  6.5 0.0 copy-start
  6.5 0.0 copy-start.1
  6.5 0.0 copy-start.2
  6.5 0.0 all-gather.2.cloned.1.call-start
  6.5 0.7 all-gather.2.cloned.1.call-update
  7.3 1.1 copy.19
  8.3 0.8 reshape.78
  9.2 19.3 %all-to-all-start = ((bf16[64,2,512]{2,1,0:T(2,128)(2,1)}), bf16[64,2,512]{2,1,0:T(2,128)(2,1)S(1)}, u32[]{:S(2)}, u32[]{:S(2)}) async-start(bf16[64,2,512]{2,1,0:T(2,128)(2,1)} %reshape.78), calls=%async_computation | async-start | bytes 262144 | tf_op jit(solution)/shard_map/all_to_all | solution.py:56
  28.5 0.0 reduce-scatter.2.cloned.1.call-start
  28.5 2.1 reshape.77
  30.7 0.1 fusion.75
  30.8 0.1 fusion.63
  31.0 12.4 %all-to-all-done = bf16[64,2,512]{2,1,0:T(2,128)(2,1)S(1)} async-done(((bf16[64,2,512]{2,1,0:T(2,128)(2,1)}), bf16[64,2,512]{2,1,0:T(2,128)(2,1)S(1)}, u32[]{:S(2)}, u32[]{:S(2)}) %all-to-all-start) | async-done | bytes 131104 | tf_op jit(solution)/shard_map/all_to_all | solution.py:56
  43.4 0.2 reshape.79
  43.6 0.3 copy.20
  43.9 0.5 fusion.83
  44.4 0.5 fusion.80
  44.9 0.7 fusion.12
  45.7 0.7 fusion.8
  46.4 0.8 fusion.2
  47.2 0.9 multiply_add_fusion
  48.1 0.7 fusion.45
  48.8 0.7 fusion.39
  49.5 0.7 convolution_subtract_fusion.1
  50.3 0.7 convolution_add_fusion
  51.0 1.7 fusion.6
  52.7 1.7 fusion.4
  54.4 0.2 copy.28
  54.6 0.2 reshape.80
  54.8 24.2 %all_to_all.26 = bf16[64,2,512]{2,1,0:T(2,128)(2,1)S(1)} all-to-all(bf16[64,2,512]{2,1,0:T(2,128)(2,1)S(1)} %reshape.80), channel_id=1, replica_groups=mesh['seq'=64,'chan'=8] {'seq'}, dimensions={0} | all-to-all | bytes 262144 | tf_op jit(solution)/shard_map/all_to_all | solution.py:58
  79.0 0.2 reshape.81
  79.2 0.2 copy.23
  79.4 150.3 %all-gather.2.cloned.1.call-done = bf16[1024,8192]{1,0:T(8,128)(2,1)} async-done(((bf16[1024,128]{1,0:T(8,128)(2,1)}), bf16[1024,8192]{1,0:T(8,128)(2,1)}) %all-gather.2.cloned.1.call-update) | async-done | bytes 16777232 | tf_op jit(solution)/shard_map/all_gather | solution.py:65
  229.7 0.0 copy-done
  229.7 0.0 copy-done.1
  229.7 0.0 copy-done.2
  229.7 9.8 %convolution_convert_fusion = bf16[64,8192]{1,0:T(8,128)(2,1)} fusion(bf16[1024,8192]{1,0:T(8,128)(2,1)} %all-gather.2.cloned.1.call-done, f32[1024,64]{0,1:T(8,128)S(1)} %copy.23, bf16[64,1024]{1,0:T(8,128)(2,1)S(1)} %copy-done, bf16[64,1024]{1,0:T(8,128)(2,1)S(1)} %copy-done.1, f32[1024]{0:T(1024)S(1)} %copy-done.2), kind=kOutput, calls=%fused_computation | convolution fusion | flops 1074659328 | bytes 18354176 | tf_op jit(solution)/shard_map/dot_general | solution.py:63
  239.5 0.0 reduce-scatter.2.cloned.1.call-update
  239.5 39.6 %reduce-scatter.2.cloned.1.call-done = bf16[64,1024]{1,0:T(8,128)(2,1)} async-done(((bf16[64,8192]{1,0:T(8,128)(2,1)}), bf16[64,1024]{1,0:T(8,128)(2,1)}) %reduce-scatter.2.cloned.1.call-update) | async-done | bytes 131088 | tf_op jit(solution)/shard_map/reduce_scatter | solution.py:68
  (1 shorter events, 0.0 us)
Async XLA Ops:
  6.5 223.2 %copy-start = (bf16[64,1024]{1,0:T(8,128)(2,1)S(1)}, bf16[64,1024]{1,0:T(8,128)(2,1)}, u32[]{:S(2)}) copy-start(bf16[64,1024]{1,0:T(8,128)(2,1)} %param.5) | copy-start | bytes 393220
  6.5 223.2 %copy-start.1 = (bf16[64,1024]{1,0:T(8,128)(2,1)S(1)}, bf16[64,1024]{1,0:T(8,128)(2,1)}, u32[]{:S(2)}) copy-start(bf16[64,1024]{1,0:T(8,128)(2,1)} %param.6) | copy-start | bytes 393220
  6.5 223.2 %copy-start.2 = (f32[1024]{0:T(1024)S(1)}, f32[1024]{0:T(1024)}, u32[]{:S(2)}) copy-start(f32[1024]{0:T(1024)} %param.8) | copy-start | bytes 12292
  6.5 223.2 %all-gather.2.cloned.1.call-start = ((), (), s32[]{:S(2)}) async-start(), calls=%async_computation.3 | async-start | bytes 17039360 | tf_op jit(solution)/shard_map/all_gather | solution.py:65
  9.2 34.2 %all-to-all-start = ((bf16[64,2,512]{2,1,0:T(2,128)(2,1)}), bf16[64,2,512]{2,1,0:T(2,128)(2,1)S(1)}, u32[]{:S(2)}, u32[]{:S(2)}) async-start(bf16[64,2,512]{2,1,0:T(2,128)(2,1)} %reshape.78), calls=%async_computation | async-start | bytes 262144 | tf_op jit(solution)/shard_map/all_to_all | solution.py:56
  28.5 250.6 %reduce-scatter.2.cloned.1.call-start = ((), (), s32[]{:S(2)}) async-start(), calls=%async_computation.4 | async-start | bytes 1179648 | tf_op jit(solution)/shard_map/reduce_scatter | solution.py:68
Sparse Core Ops, SparseCore 0:
  10.3 219.3 all-gather.1
  239.6 39.4 reduce-scatter.1
where the time goes:
time: 287 us; the launch traced here: 286 us
  waiting for transfers between devices  203 us (71%)
  blocking collectives  24.2 us (8%)
  matrix products  20.2 us (7%)
  starting transfers between devices  19.3 us (7%)
  between operations  13.6 us (5%)
  local copies, waits for them, and re-layouts  5.32 us (2%)
    all_gather x1, waiting for transfers between devices, per_device(): lax.all_gather(out_weight, 'seq', axis=1, tiled=True)  150 us
    reduce_scatter x1, waiting for transfers between devices, per_device(): lax.psum_scatter(partial_terms.astype(jnp.bfloat16), 'chan', scatter_dime...  39.6 us
    all_to_all x1, blocking collectives, per_device(): lax.all_to_all(conv, 'seq', split_axis=1, concat_axis=0, tiled=True)  24.2 us
    all_to_all x1, starting transfers between devices, per_device(): lax.all_to_all(values_t, 'seq', split_axis=0, concat_axis=1, tiled=True)  19.3 us
    all_to_all x1, waiting for transfers between devices, per_device(): lax.all_to_all(values_t, 'seq', split_axis=0, concat_axis=1, tiled=True)  12.4 us
    dot_general x1, matrix products, per_device(): jnp.dot(gated, lax.all_gather(out_weight, 'seq', axis=1, tiled=True), pre...  9.77 us
    dot_general x10, matrix products, mult(): return jnp.einsum(form, left, right, precision=high)  9.46 us
  transfers between devices with their start and end apart: 3, of which 3 were waited for; matrix products, arithmetic and copies ran while one was open for 6% of the time, Pallas kernels for 0%

commit v1 on v0

v1 whole, which is shorter than its diff:
```python
import jax
import jax.numpy as jnp
import numpy as np
from jax import lax
from jax.experimental import pallas as pl
from jax.experimental.pallas import tpu as pltpu
from jax.sharding import Mesh, PartitionSpec as P

Z, Y, X, CORE = 16, 4, 4, 2
HALF = 64
TALL = 128
FFT = 8192


def split(table):
    top = table.astype(jnp.bfloat16)
    rest = (table - top.astype(np.float64)).astype(jnp.bfloat16)
    return top, rest


def fft_tables():
    turn = 2.0 * np.pi
    k, s, m = np.arange(TALL), np.arange(HALF), np.arange(HALF)
    one = turn * (np.outer(k, s) % TALL) / TALL
    first = np.concatenate([np.cos(one), np.sin(one)], 0)
    first = np.concatenate(split(first), 1)
    spin = turn * np.outer(k, m) / FFT
    cos, sin = np.cos(spin), np.sin(spin)
    fwd = np.stack([np.concatenate([cos, -sin], 1), np.concatenate([-sin, -cos], 1)])
    inv = np.stack([np.concatenate([cos, cos], 1), np.concatenate([-sin, sin], 1)])
    two = turn * (np.outer(m, m) % HALF) / HALF
    c2, s2 = np.cos(two), np.sin(two)
    ahead = np.block([[c2, -s2, -s2, c2], [s2, c2, c2, s2]])
    back = np.block([[c2, s2, s2, c2], [-s2, c2, c2, -s2]])

    def triple(table):
        top, rest = split(table)
        return np.concatenate([top, top, rest], 0)

    four = turn * (np.outer(s, k) % TALL) / TALL
    last = np.concatenate([np.cos(four), -np.sin(four)], 0) / FFT
    top, rest = split(last)
    last = np.concatenate([top, top, rest], 1)
    return (
        first,
        np.concatenate([fwd, inv]).astype(np.float32),
        np.stack([triple(ahead), triple(back)]),
        last,
    )


def pieces(value):
    top = value.astype(jnp.bfloat16)
    rest = (value - top.astype(jnp.float32)).astype(jnp.bfloat16)
    return [top, rest, top]


def conv_kernel(sig_ref, spec_ref, first_ref, spin_ref, mid_ref, last_ref, out_ref):
    width = 2 * HALF
    left = lax.broadcasted_iota(jnp.int32, (1, width), 1) < HALF
    fp, fq, ip, iq = [spin_ref[i] for i in range(4)]

    def swap(value):
        return pltpu.roll(value, HALF, 1)

    def dot(one, two):
        return jnp.dot(one, two, preferred_element_type=jnp.float32)

    for pair in range(sig_ref.shape[1] // width):
        lanes = slice(pair * width, (pair + 1) * width)
        data = sig_ref[:, lanes].astype(jnp.float32)
        other = swap(data)
        wide = jnp.concatenate([jnp.where(left, data, other), jnp.where(left, other, data)], 1)
        wide = wide.astype(jnp.bfloat16)
        both = dot(first_ref[...], jnp.concatenate([wide, wide], 0))
        turned = jnp.concatenate(
            [
                both[:TALL, c * width : (c + 1) * width] * fp + both[TALL:, c * width : (c + 1) * width] * fq
                for c in range(2)
            ],
            0,
        )
        freq = dot(jnp.concatenate(pieces(turned), 1), mid_ref[0])
        filt = jnp.concatenate([spec_ref[2 * pair + c].T for c in range(2)], 0)
        turned_filt = swap(filt)
        prod = freq[:, :width] * jnp.where(left, filt, turned_filt) + freq[:, width:] * jnp.where(
            left, -turned_filt, filt
        )
        back = dot(jnp.concatenate(pieces(prod), 1), mid_ref[1])
        spun = jnp.concatenate(
            [
                back[c * TALL : (c + 1) * TALL, :width] * ip + back[c * TALL : (c + 1) * TALL, width:] * iq
                for c in range(2)
            ],
            1,
        )
        ends = dot(last_ref[...], jnp.concatenate(pieces(spun), 0))
        even, odd = ends[:, :width], ends[:, width:]
        conv = jnp.where(left, even[:HALF], odd[HALF:]) + swap(jnp.where(left, odd[:HALF], even[HALF:]))
        out_ref[:, lanes] = conv.astype(jnp.bfloat16)


def long_conv(sig, spec):
    tables = fft_tables()
    vmem = pl.BlockSpec(memory_space=pltpu.VMEM)
    return pl.pallas_call(
        conv_kernel,
        out_shape=jax.ShapeDtypeStruct(sig.shape, jnp.bfloat16),
        in_specs=[vmem] * 6,
        out_specs=vmem,
        compiler_params=pltpu.CompilerParams(vmem_limit_bytes=32 * 1024 * 1024),
        cost_estimate=pl.CostEstimate(flops=1_200_000_000, bytes_accessed=2_000_000, transcendentals=0),
        name="long_conv",
    )(sig, spec, *[jnp.asarray(t) for t in tables])


def turn_kernel(left_ref, out_ref):
    near, far = left_ref.shape[:2]
    blocks = [left_ref[a, b] for b in range(far) for a in range(near)]
    out_ref[...] = jnp.concatenate(blocks, 0).T


def turn(left):
    near, far, width, tokens = left.shape
    vmem = pl.BlockSpec(memory_space=pltpu.VMEM)
    return pl.pallas_call(
        turn_kernel,
        out_shape=jax.ShapeDtypeStruct((tokens, near * far * width), jnp.bfloat16),
        in_specs=[vmem],
        out_specs=vmem,
        compiler_params=pltpu.CompilerParams(vmem_limit_bytes=16 * 1024 * 1024),
        name="turn",
    )(left)


def project_kernel(left_ref, weight_ref, out_ref, held_ref, sems):
    blocks, _, cols = weight_ref.shape
    copies = [pltpu.make_async_copy(weight_ref.at[i], held_ref.at[i], sems.at[i]) for i in range(blocks)]
    for copy in copies:
        copy.start()
    left = left_ref[...]
    step = blocks // (X * CORE)
    for i in range(X * CORE):
        for p in range(step):
            copies[i * step + p].wait()
        weight = jnp.concatenate([held_ref[i * step + p] for p in range(step)], 1)
        part = jnp.dot(left, weight, preferred_element_type=jnp.float32).astype(jnp.bfloat16)
        out_ref[i % CORE, :, i // CORE] = part.reshape(out_ref.shape[1], HALF, step * cols)


def project(left, weight):
    tokens, depth = left.shape
    blocks, _, cols = weight.shape
    wide = blocks // (X * CORE) * cols
    vmem = pl.BlockSpec(memory_space=pltpu.VMEM)
    return pl.pallas_call(
        project_kernel,
        out_shape=jax.ShapeDtypeStruct((CORE, tokens // HALF, X, HALF, wide), jnp.bfloat16),
        in_specs=[vmem, pl.BlockSpec(memory_space=pl.ANY)],
        out_specs=vmem,
        scratch_shapes=[pltpu.VMEM(weight.shape, weight.dtype), pltpu.SemaphoreType.DMA((blocks,))],
        compiler_params=pltpu.CompilerParams(vmem_limit_bytes=52 * 1024 * 1024),
        cost_estimate=pl.CostEstimate(flops=2 * depth * tokens * blocks * cols, bytes_accessed=6_000_000, transcendentals=0),
        name="project",
    )(left, weight)


def gather_kernel(part_ref, out_ref):
    cols = out_ref.shape[1] // (part_ref.shape[0] * 2)
    for y in range(part_ref.shape[0]):
        total = part_ref[y, 0].astype(jnp.float32)
        for x in range(1, part_ref.shape[1]):
            total = total + part_ref[y, x].astype(jnp.float32)
        total = total.astype(jnp.bfloat16)
        for p in range(2):
            at = (p * part_ref.shape[0] + y) * cols
            out_ref[:, at : at + cols] = total[:, p * cols : (p + 1) * cols]


def gather(part):
    vmem = pl.BlockSpec(memory_space=pltpu.VMEM)
    return pl.pallas_call(
        gather_kernel,
        out_shape=jax.ShapeDtypeStruct((part.shape[2], part.shape[0] * part.shape[3]), jnp.bfloat16),
        in_specs=[vmem],
        out_specs=vmem,
        compiler_params=pltpu.CompilerParams(vmem_limit_bytes=16 * 1024 * 1024),
        name="gather",
    )(part)


def per_device(values, gate, spectrum, bias, out_weight):
    rows, group = values.shape
    width = group // (Z * Y)
    cols = out_weight.shape[1]
    weight = lax.all_gather(out_weight, "z", axis=0, tiled=False)

    def by_y(array):
        return array.T.reshape(Z, Y, width, rows).transpose(1, 0, 2, 3).reshape(Y, Z, width * rows)

    near = jnp.concatenate([by_y(values), by_y(gate)], axis=1)
    near = lax.all_to_all(near, "y", split_axis=0, concat_axis=0, tiled=True)
    sig, gat = near[:, :Z], near[:, Z:]
    moved = lax.all_to_all(sig.transpose(1, 0, 2), "z", split_axis=0, concat_axis=0, tiled=True)
    conv = long_conv(moved.reshape(Z * Y, width * rows), spectrum.reshape(width, TALL, TALL))
    conv = lax.all_to_all(conv.reshape(Z, Y, width * rows), "z", split_axis=0, concat_axis=0, tiled=True)
    skip = lax.dynamic_index_in_dim(bias.reshape(Z, Y, width), lax.axis_index("y"), 1, keepdims=False)
    skip = jnp.broadcast_to(skip[:, :, None], (Z, width, rows)).reshape(Z, width * rows)
    conv = conv.transpose(1, 0, 2).astype(jnp.float32)
    gated = (gat.astype(jnp.float32) * (conv + skip[None] * sig.astype(jnp.float32))).astype(jnp.bfloat16)

    left = gated.reshape(Y, Z, width, rows).transpose(1, 2, 0, 3).reshape(Z, width, Y * rows)
    wide = jnp.broadcast_to(left[None], (Y,) + left.shape)
    wide = lax.all_to_all(wide, "y", split_axis=0, concat_axis=0, tiled=True)

    part = project(turn(wide), weight)
    part = lax.all_to_all(part, "core", split_axis=0, concat_axis=0, tiled=True)
    part = (part[0].astype(jnp.float32) + part[1].astype(jnp.float32)).astype(jnp.bfloat16)
    part = part.reshape((Y * X,) + part.shape[2:])
    part = lax.all_to_all(part, ("y", "x"), split_axis=0, concat_axis=0, tiled=True)
    return gather(part.reshape(Y, X, rows, -1))


def solution(mesh):
    names = ("z", "y", "x", "core")
    fine = Mesh(mesh.devices.reshape(Z, Y, X, CORE), names)
    seq, chan = names[:2], names[2:]
    placed = (
        P(seq, chan),
        P(seq, chan),
        P(chan + seq, None, None),
        P(chan),
        P(chan, seq),
    )
    return jax.shard_map(
        per_device, mesh=fine, in_specs=placed, out_specs=P(seq, chan), check_vma=False
    )
```

time: 287 us -> 137 us (0.48)
  waiting for transfers between devices: 203 us -> 36.9 us
  blocking collectives: 24.2 us -> 49.1 us
  matrix products: 20.2 us -> 0 us
  Pallas kernels: 0 us -> 10.1 us
    all_gather x1, waiting for transfers between devices: 150 us -> 12 us  [per_device(): weight = lax.all_gather(out_weight, 'z', axis=0, tiled=False)]
    reduce_scatter x1 -> x0, waiting for transfers between devices: 39.6 us -> none  [per_device(): lax.psum_scatter(partial_terms.astype(jnp.bfloat16), 'chan', scatter_dime...]
    all_to_all x1 -> x4, blocking collectives: 24.2 us -> 49.1 us  [the longest x1 16.6 us: per_device(): lax.all_to_all(part, ('y', 'x'), split_axis=0, concat_axis=0, tiled=True)]
    dot_general x11 -> x0, matrix products: 19.2 us -> none  [the longest x1 9.77 us: per_device(): jnp.dot(gated, lax.all_gather(out_weight, 'seq', axis=1, tiled=True), pre...]
    all_to_all x1 -> x2, waiting for transfers between devices: 12.4 us -> 24.2 us  [the longest x1 12.5 us: per_device(): lax.all_to_all(conv.reshape(Z, Y, width * rows), 'z', split_axis=0, conca...]
    pallas_call x0 -> x4, Pallas kernels: none -> 10.1 us  [the longest x1 4.68 us: long_conv(): pl.pallas_call(conv_kernel, out_shape=jax.ShapeDtypeStruct(sig.shape, jnp...]
    all_to_all x1 -> x2, starting transfers between devices: 19.3 us -> 20.9 us  [the longest x1 14.9 us: per_device(): lax.all_to_all(sig.transpose(1, 0, 2), 'z', split_axis=0, concat_axis=0,...]
  transfers between devices with their start and end apart: 3 -> 3, of which waited for: 3 -> 3; matrix products, arithmetic and copies ran while one was open for 6% -> 4% of each run, Pallas kernels for 0% -> 4%
where the time goes in v1:
time: 137 us
  blocking collectives  49.1 us (36%)
  waiting for transfers between devices  36.9 us (27%)
  starting transfers between devices  21 us (15%)
  between operations  13.6 us (10%)
  Pallas kernels  10.1 us (7%)
  local copies, waits for them, and re-layouts  5.98 us (4%)
    all_to_all x1, blocking collectives, per_device(): lax.all_to_all(part, ('y', 'x'), split_axis=0, concat_axis=0, tiled=True)  16.6 us
    all_to_all x1, starting transfers between devices, per_device(): lax.all_to_all(sig.transpose(1, 0, 2), 'z', split_axis=0, concat_axis=0,...  14.9 us
    all_to_all x1, blocking collectives, per_device(): part = lax.all_to_all(part, 'core', split_axis=0, concat_axis=0, tiled=True)  12.7 us
    all_to_all x1, waiting for transfers between devices, per_device(): lax.all_to_all(conv.reshape(Z, Y, width * rows), 'z', split_axis=0, conca...  12.5 us
    all_gather x1, waiting for transfers between devices, per_device(): weight = lax.all_gather(out_weight, 'z', axis=0, tiled=False)  12 us
    all_to_all x1, waiting for transfers between devices, per_device(): lax.all_to_all(sig.transpose(1, 0, 2), 'z', split_axis=0, concat_axis=0,...  11.7 us
    all_to_all x1, blocking collectives, per_device(): near = lax.all_to_all(near, 'y', split_axis=0, concat_axis=0, tiled=True)  10.3 us
    all_to_all x1, blocking collectives, per_device(): wide = lax.all_to_all(wide, 'y', split_axis=0, concat_axis=0, tiled=True)  9.5 us
  transfers between devices with their start and end apart: 3, of which 3 were waited for; matrix products, arithmetic and copies ran while one was open for 4% of the time, Pallas kernels for 4%

profile of v1, /device:TPU:1, one launch (start us, length us, event | category | flops | bytes accessed | tf_op | source)
XLA Modules:
  0.0 136.9 jit_solution(483182103327001474)
XLA Ops:
  6.5 0.0 copy-start.3
  6.5 0.0 copy-start.1
  6.5 0.0 copy-start
  6.5 0.0 copy-start.2
  6.5 0.0 copy-start.4
  6.5 0.0 all-gather.3.cloned.1.call-start
  6.6 0.7 all-gather.3.cloned.1.call-update
  7.3 1.1 copy.23
  8.4 0.2 reshape.42
  8.6 1.1 copy.24
  9.7 0.2 reshape.44
  10.0 0.0 copy-start.5
  10.0 10.3 %all_to_all.30 = bf16[4,32,1024]{2,1,0:T(8,128)(2,1)S(1)} all-to-all(bf16[4,32,1024]{2,1,0:T(8,128)(2,1)S(1)} %pad_maximum_fusion), channel_id=1, replica_groups=mesh['z'=16,'y'=4,'x'=4,'core'=2] {'y'}, dimensions={0} | all-to-all | bytes 524288 | tf_op jit(solution)/shard_map/all_to_all | solution.py:202
  20.3 0.8 copy.27
  21.1 14.9 %all-to-all-start.1 = ((bf16[16,4,1024]{2,1,0:T(4,128)(2,1)}), bf16[16,4,1024]{2,1,0:T(4,128)(2,1)S(1)}, u32[]{:S(2)}, u32[]{:S(2)}) async-start(bf16[16,4,1024]{2,1,0:T(4,128)(2,1)} %copy.27), calls=%async_computation.1 | async-start | bytes 262144 | tf_op jit(solution)/shard_map/all_to_all | solution.py:204
  36.1 0.0 copy-done.4
  36.1 0.9 reshape.46.spec_ref
  37.0 11.7 %all-to-all-done.1 = bf16[16,4,1024]{2,1,0:T(4,128)(2,1)S(1)} async-done(((bf16[16,4,1024]{2,1,0:T(4,128)(2,1)}), bf16[16,4,1024]{2,1,0:T(4,128)(2,1)S(1)}, u32[]{:S(2)}, u32[]{:S(2)}) %all-to-all-start.1) | async-done | bytes 131104 | tf_op jit(solution)/shard_map/all_to_all | solution.py:204
  48.7 0.0 copy-done.3
  48.8 0.0 copy-done.1
  48.8 0.0 copy-done
  48.8 0.0 copy-done.2
  48.8 4.7 %long_conv.1 = bf16[64,1024]{1,0:T(8,128)(2,1)S(1)} custom-call(bf16[64,1024]{1,0:T(8,128)(2,1)S(1)} %reshape.45.sig_ref, f32[16,128,128]{2,1,0:T(8,128)S(1)} %reshape.46.spec_ref, bf16[256,128]{1,0:T(8,128)(2,1)S(1)} %copy-done.3, f32[4,128,128]{2,1,0:T(8,128)S(1)} %copy-done.1, bf16[2,384,256]{2,1,0:T(8,128)(2,1)S(1)} %copy-done, ...), custom_call_target="tpu_custom_call" | custom-call | flops 1200000000 | bytes 2000000 | tf_op jit(solution)/shard_map/long_conv/pallas_call | solution.py:106
  53.5 0.7 reshape.47
  54.2 6.0 %all-to-all-start.2 = ((bf16[16,4,1024]{2,1,0:T(4,128)(2,1)}), bf16[16,4,1024]{2,1,0:T(4,128)(2,1)S(1)}, u32[]{:S(2)}, u32[]{:S(2)}) async-start(bf16[16,4,1024]{2,1,0:T(4,128)(2,1)} %reshape.47), calls=%async_computation.2 | async-start | bytes 262144 | tf_op jit(solution)/shard_map/all_to_all | solution.py:206
  60.2 0.0 copy-done.5
  60.2 0.1 reshape.48
  60.3 0.1 broadcast_in_dim.16
  60.4 0.1 mul.13
  60.5 12.5 %all-to-all-done.2 = bf16[16,4,1024]{2,1,0:T(4,128)(2,1)S(1)} async-done(((bf16[16,4,1024]{2,1,0:T(4,128)(2,1)}), bf16[16,4,1024]{2,1,0:T(4,128)(2,1)S(1)}, u32[]{:S(2)}, u32[]{:S(2)}) %all-to-all-start.2) | async-done | bytes 131104 | tf_op jit(solution)/shard_map/all_to_all | solution.py:206
  73.0 0.1 fusion.1
  73.0 0.2 reshape.49
  73.2 0.2 copy.29
  73.4 0.2 broadcast_in_dim.17
  73.7 9.5 %all_to_all.31.left_ref = bf16[4,16,16,256]{3,2,1,0:T(8,128)(2,1)S(1)} all-to-all(bf16[4,16,16,256]{3,2,1,0:T(8,128)(2,1)S(1)} %broadcast_in_dim.18), channel_id=1, replica_groups=mesh['z'=16,'y'=4,'x'=4,'core'=2] {'y'}, dimensions={0} | all-to-all | bytes 1048576 | tf_op jit(solution)/shard_map/all_to_all | solution.py:214
  83.2 0.2 turn.1.left_ref
  83.4 12.0 %all-gather.3.cloned.1.call-done = bf16[16384,128]{1,0:T(8,128)(2,1)} async-done(((bf16[1024,128]{1,0:T(8,128)(2,1)}), bf16[16384,128]{1,0:T(8,128)(2,1)}) %all-gather.3.cloned.1.call-update) | async-done | bytes 4194320 | tf_op jit(solution)/shard_map/all_gather | solution.py:196
  95.4 4.5 %project.1 = bf16[2,4,4,64,256]{4,3,2,1,0:T(8,128)(2,1)S(1)} custom-call(bf16[256,1024]{1,0:T(8,128)(2,1)S(1)} %turn.1.left_ref, bf16[16,1024,128]{2,1,0:T(8,128)(2,1)} %bitcast.32), custom_call_target="tpu_custom_call" | custom-call | flops 1073741824 | bytes 6000000 | tf_op jit(solution)/shard_map/project/pallas_call | solution.py:156
  99.9 12.7 %all_to_all.32 = bf16[2,4,4,64,256]{4,3,2,1,0:T(8,128)(2,1)S(1)} all-to-all(bf16[2,4,4,64,256]{4,3,2,1,0:T(8,128)(2,1)S(1)} %project.1), channel_id=1, replica_groups=mesh['z'=16,'y'=4,'x'=4,'core'=2] {'core'}, dimensions={0} | all-to-all | bytes 2097152 | tf_op jit(solution)/shard_map/all_to_all | solution.py:217
  112.6 0.2 add_convert_fusion
  112.7 16.6 %all_to_all.33 = bf16[16,64,256]{2,1,0:T(8,128)(2,1)S(1)} all-to-all(bf16[16,64,256]{2,1,0:T(8,128)(2,1)S(1)} %bitcast.33), channel_id=1, replica_groups=mesh['z'=16,'y'=4,'x'=4,'core'=2] {'y','x'}, dimensions={0} | all-to-all | bytes 1048576 | tf_op jit(solution)/shard_map/all_to_all | solution.py:220
  129.3 0.7 gather.1
  (7 shorter events, 0.2 us)
Async XLA Ops:
  6.5 42.2 %copy-start.3 = (bf16[256,128]{1,0:T(8,128)(2,1)S(1)}, bf16[256,128]{1,0:T(8,128)(2,1)}, u32[]{:S(2)}) copy-start(bf16[256,128]{1,0:T(8,128)(2,1)} %constant.19.clone.first_ref) | copy-start | bytes 196612
  6.5 42.2 %copy-start.1 = (f32[4,128,128]{2,1,0:T(8,128)S(1)}, f32[4,128,128]{2,1,0:T(8,128)}, u32[]{:S(2)}) copy-start(f32[4,128,128]{2,1,0:T(8,128)} %constant.20.clone.spin_ref) | copy-start | bytes 786436
  6.5 42.2 %copy-start = (bf16[2,384,256]{2,1,0:T(8,128)(2,1)S(1)}, bf16[2,384,256]{2,1,0:T(8,128)(2,1)}, u32[]{:S(2)}) copy-start(bf16[2,384,256]{2,1,0:T(8,128)(2,1)} %constant.21.clone.mid_ref) | copy-start | bytes 1179652
  6.5 42.2 %copy-start.2 = (bf16[128,384]{1,0:T(8,128)(2,1)S(1)}, bf16[128,384]{1,0:T(8,128)(2,1)}, u32[]{:S(2)}) copy-start(bf16[128,384]{1,0:T(8,128)(2,1)} %constant.22.clone.last_ref) | copy-start | bytes 294916
  6.5 29.5 %copy-start.4 = (f32[16,2,8192]{2,1,0:T(2,128)S(1)}, f32[16,2,8192]{2,1,0:T(2,128)}, u32[]{:S(2)}) copy-start(f32[16,2,8192]{2,1,0:T(2,128)} %param.11) | copy-start | bytes 3145732
  6.5 88.8 %all-gather.3.cloned.1.call-start = ((), (), s32[]{:S(2)}) async-start(), calls=%async_computation.6 | async-start | bytes 4456448 | tf_op jit(solution)/shard_map/all_gather | solution.py:196
  10.0 50.2 %copy-start.5 = (f32[1024]{0:T(1024)S(1)}, f32[1024]{0:T(1024)}, u32[]{:S(2)}) copy-start(f32[1024]{0:T(1024)} %param.12) | copy-start | bytes 12292
  21.1 27.6 %all-to-all-start.1 = ((bf16[16,4,1024]{2,1,0:T(4,128)(2,1)}), bf16[16,4,1024]{2,1,0:T(4,128)(2,1)S(1)}, u32[]{:S(2)}, u32[]{:S(2)}) async-start(bf16[16,4,1024]{2,1,0:T(4,128)(2,1)} %copy.27), calls=%async_computation.1 | async-start | bytes 262144 | tf_op jit(solution)/shard_map/all_to_all | solution.py:204
  54.2 18.8 %all-to-all-start.2 = ((bf16[16,4,1024]{2,1,0:T(4,128)(2,1)}), bf16[16,4,1024]{2,1,0:T(4,128)(2,1)S(1)}, u32[]{:S(2)}, u32[]{:S(2)}) async-start(bf16[16,4,1024]{2,1,0:T(4,128)(2,1)} %reshape.47), calls=%async_computation.2 | async-start | bytes 262144 | tf_op jit(solution)/shard_map/all_to_all | solution.py:206
Sparse Core Ops, SparseCore 0:
  9.5 85.8 all-gather.2

commit v2 on v1

--- a/solution.py
+++ b/solution.py
@@ -133,36 +133,40 @@
     )(left)
 
 
-def project_kernel(left_ref, weight_ref, out_ref, held_ref, sems):
+def project_kernel(me_ref, left_ref, weight_ref, keep_ref, send_ref, held_ref, sems):
     blocks, _, cols = weight_ref.shape
     copies = [pltpu.make_async_copy(weight_ref.at[i], held_ref.at[i], sems.at[i]) for i in range(blocks)]
     for copy in copies:
         copy.start()
     left = left_ref[...]
-    step = blocks // (X * CORE)
-    for i in range(X * CORE):
+    step = blocks // X
+    pair = step // CORE
+    mine = me_ref[0]
+    for x in range(X):
         for p in range(step):
-            copies[i * step + p].wait()
-        weight = jnp.concatenate([held_ref[i * step + p] for p in range(step)], 1)
+            copies[x * step + p].wait()
+        order = [x * step + core * pair + p for core in (mine, 1 - mine) for p in range(pair)]
+        weight = jnp.concatenate([held_ref[i] for i in order], 1)
         part = jnp.dot(left, weight, preferred_element_type=jnp.float32).astype(jnp.bfloat16)
-        out_ref[i % CORE, :, i // CORE] = part.reshape(out_ref.shape[1], HALF, step * cols)
-
-
-def project(left, weight):
+        keep_ref[:, x] = part[:, : pair * cols].reshape(keep_ref.shape[0], HALF, pair * cols)
+        send_ref[:, x] = part[:, pair * cols :].reshape(keep_ref.shape[0], HALF, pair * cols)
+
+
+def project(me, left, weight):
     tokens, depth = left.shape
     blocks, _, cols = weight.shape
     wide = blocks // (X * CORE) * cols
     vmem = pl.BlockSpec(memory_space=pltpu.VMEM)
     return pl.pallas_call(
         project_kernel,
-        out_shape=jax.ShapeDtypeStruct((CORE, tokens // HALF, X, HALF, wide), jnp.bfloat16),
-        in_specs=[vmem, pl.BlockSpec(memory_space=pl.ANY)],
-        out_specs=vmem,
+        out_shape=[jax.ShapeDtypeStruct((tokens // HALF, X, HALF, wide), jnp.bfloat16)] * 2,
+        in_specs=[pl.BlockSpec(memory_space=pltpu.SMEM), vmem, pl.BlockSpec(memory_space=pl.ANY)],
+        out_specs=[vmem, vmem],
         scratch_shapes=[pltpu.VMEM(weight.shape, weight.dtype), pltpu.SemaphoreType.DMA((blocks,))],
         compiler_params=pltpu.CompilerParams(vmem_limit_bytes=52 * 1024 * 1024),
         cost_estimate=pl.CostEstimate(flops=2 * depth * tokens * blocks * cols, bytes_accessed=6_000_000, transcendentals=0),
         name="project",
-    )(left, weight)
+    )(me, left, weight)
 
 
 def gather_kernel(part_ref, out_ref):
@@ -213,9 +217,10 @@
     wide = jnp.broadcast_to(left[None], (Y,) + left.shape)
     wide = lax.all_to_all(wide, "y", split_axis=0, concat_axis=0, tiled=True)
 
-    part = project(turn(wide), weight)
-    part = lax.all_to_all(part, "core", split_axis=0, concat_axis=0, tiled=True)
-    part = (part[0].astype(jnp.float32) + part[1].astype(jnp.float32)).astype(jnp.bfloat16)
+    me = lax.axis_index("core").astype(jnp.int32).reshape(1)
+    keep, send = project(me, turn(wide), weight)
+    other = lax.ppermute(send, "core", [(0, 1), (1, 0)])
+    part = (keep.astype(jnp.float32) + other.astype(jnp.float32)).astype(jnp.bfloat16)
     part = part.reshape((Y * X,) + part.shape[2:])
     part = lax.all_to_all(part, ("y", "x"), split_axis=0, concat_axis=0, tiled=True)
     return gather(part.reshape(Y, X, rows, -1))

time: 137 us -> 135 us (0.985)
  blocking collectives: 49.1 us -> 26.8 us
  starting transfers between devices: 21 us -> 35 us
  waiting for transfers between devices: 36.9 us -> 43.6 us
  Pallas kernels: 10.1 us -> 8.7 us
    all_to_all x2 -> x0, blocking collectives: 22.2 us -> none  [the longest x1 12.7 us: per_device(): part = lax.all_to_all(part, 'core', split_axis=0, concat_axis=0, tiled=True)]
    ppermute x0 -> x1, starting transfers between devices: none -> 10.5 us  [per_device(): other = lax.ppermute(send, 'core', [(0, 1), (1, 0)])]
    all_to_all x0 -> x1, waiting for transfers between devices: none -> 6.94 us  [per_device(): wide = lax.all_to_all(wide, 'y', split_axis=0, concat_axis=0, tiled=True)]
    all_to_all x0 -> x1, starting transfers between devices: none -> 3.47 us  [per_device(): wide = lax.all_to_all(wide, 'y', split_axis=0, concat_axis=0, tiled=True)]
    all_gather x1, waiting for transfers between devices: 12 us -> 10.3 us  [per_device(): weight = lax.all_gather(out_weight, 'z', axis=0, tiled=False)]
    ppermute x0 -> x1, waiting for transfers between devices: none -> 1.51 us  [per_device(): other = lax.ppermute(send, 'core', [(0, 1), (1, 0)])]
    pallas_call x1, Pallas kernels: 4.55 us -> 3.1 us  [project(): pl.pallas_call(project_kernel, out_shape=[jax.ShapeDtypeStruct((tokens //...]
  transfers between devices with their start and end apart: 3 -> 5, of which waited for: 3 -> 5; matrix products, arithmetic and copies ran while one was open for 4% -> 5% of each run, Pallas kernels for 4% -> 4%
where the time goes in v2:
time: 135 us
  waiting for transfers between devices  43.6 us (32%)
  starting transfers between devices  35 us (26%)
  blocking collectives  26.8 us (20%)
  between operations  13.6 us (10%)
  Pallas kernels  8.7 us (6%)
  local copies, waits for them, and re-layouts  6.79 us (5%)
    all_to_all x1, blocking collectives, per_device(): lax.all_to_all(part, ('y', 'x'), split_axis=0, concat_axis=0, tiled=True)  16.4 us
    all_to_all x1, starting transfers between devices, per_device(): lax.all_to_all(sig.transpose(1, 0, 2), 'z', split_axis=0, concat_axis=0,...  14.9 us
    all_to_all x1, waiting for transfers between devices, per_device(): lax.all_to_all(conv.reshape(Z, Y, width * rows), 'z', split_axis=0, conca...  12.5 us
    all_to_all x1, waiting for transfers between devices, per_device(): lax.all_to_all(sig.transpose(1, 0, 2), 'z', split_axis=0, concat_axis=0,...  11.7 us
    ppermute x1, starting transfers between devices, per_device(): other = lax.ppermute(send, 'core', [(0, 1), (1, 0)])  10.5 us
    all_to_all x1, blocking collectives, per_device(): near = lax.all_to_all(near, 'y', split_axis=0, concat_axis=0, tiled=True)  10.3 us
    all_gather x1, waiting for transfers between devices, per_device(): weight = lax.all_gather(out_weight, 'z', axis=0, tiled=False)  10.3 us
    all_to_all x1, waiting for transfers between devices, per_device(): wide = lax.all_to_all(wide, 'y', split_axis=0, concat_axis=0, tiled=True)  6.94 us
  transfers between devices with their start and end apart: 5, of which 5 were waited for; matrix products, arithmetic and copies ran while one was open for 5% of the time, Pallas kernels for 4%

profile of v2, /device:TPU:1, one launch (start us, length us, event | category | flops | bytes accessed | tf_op | source)
XLA Modules:
  0.0 134.7 jit_solution(15980826596545011677)
XLA Ops:
  6.5 0.0 copy-start.3
  6.5 0.0 copy-start.1
  6.5 0.0 copy-start
  6.5 0.0 copy-start.2
  6.5 0.0 copy-start.4
  6.5 0.0 all-gather.3.cloned.1.call-start
  6.6 0.7 all-gather.3.cloned.1.call-update
  7.3 1.1 copy.23
  8.4 0.2 reshape.42
  8.6 1.1 copy.24
  9.7 0.2 reshape.44
  10.0 0.0 copy-start.5
  10.0 10.3 %all_to_all.25 = bf16[4,32,1024]{2,1,0:T(8,128)(2,1)S(1)} all-to-all(bf16[4,32,1024]{2,1,0:T(8,128)(2,1)S(1)} %pad_maximum_fusion), channel_id=1, replica_groups=mesh['z'=16,'y'=4,'x'=4,'core'=2] {'y'}, dimensions={0} | all-to-all | bytes 524288 | tf_op jit(solution)/shard_map/all_to_all | solution.py:206
  20.3 0.8 copy.27
  21.1 14.9 %all-to-all-start.1 = ((bf16[16,4,1024]{2,1,0:T(4,128)(2,1)}), bf16[16,4,1024]{2,1,0:T(4,128)(2,1)S(1)}, u32[]{:S(2)}, u32[]{:S(2)}) async-start(bf16[16,4,1024]{2,1,0:T(4,128)(2,1)} %copy.27), calls=%async_computation.1 | async-start | bytes 262144 | tf_op jit(solution)/shard_map/all_to_all | solution.py:208
  36.1 0.0 copy-done.4
  36.1 0.9 reshape.46.spec_ref
  37.0 11.7 %all-to-all-done.1 = bf16[16,4,1024]{2,1,0:T(4,128)(2,1)S(1)} async-done(((bf16[16,4,1024]{2,1,0:T(4,128)(2,1)}), bf16[16,4,1024]{2,1,0:T(4,128)(2,1)S(1)}, u32[]{:S(2)}, u32[]{:S(2)}) %all-to-all-start.1) | async-done | bytes 131104 | tf_op jit(solution)/shard_map/all_to_all | solution.py:208
  48.7 0.0 copy-done.3
  48.8 0.0 copy-done.1
  48.8 0.0 copy-done
  48.8 0.0 copy-done.2
  48.8 4.7 %long_conv.1 = bf16[64,1024]{1,0:T(8,128)(2,1)S(1)} custom-call(bf16[64,1024]{1,0:T(8,128)(2,1)S(1)} %reshape.45.sig_ref, f32[16,128,128]{2,1,0:T(8,128)S(1)} %reshape.46.spec_ref, bf16[256,128]{1,0:T(8,128)(2,1)S(1)} %copy-done.3, f32[4,128,128]{2,1,0:T(8,128)S(1)} %copy-done.1, bf16[2,384,256]{2,1,0:T(8,128)(2,1)S(1)} %copy-done, ...), custom_call_target="tpu_custom_call" | custom-call | flops 1200000000 | bytes 2000000 | tf_op jit(solution)/shard_map/long_conv/pallas_call | solution.py:106
  53.5 0.7 reshape.47
  54.2 6.0 %all-to-all-start.2 = ((bf16[16,4,1024]{2,1,0:T(4,128)(2,1)}), bf16[16,4,1024]{2,1,0:T(4,128)(2,1)S(1)}, u32[]{:S(2)}, u32[]{:S(2)}) async-start(bf16[16,4,1024]{2,1,0:T(4,128)(2,1)} %reshape.47), calls=%async_computation.2 | async-start | bytes 262144 | tf_op jit(solution)/shard_map/all_to_all | solution.py:210
  60.2 0.0 copy-done.5
  60.2 0.1 reshape.48
  60.3 0.1 broadcast_in_dim.16
  60.4 0.1 mul.13
  60.5 12.5 %all-to-all-done.2 = bf16[16,4,1024]{2,1,0:T(4,128)(2,1)S(1)} async-done(((bf16[16,4,1024]{2,1,0:T(4,128)(2,1)}), bf16[16,4,1024]{2,1,0:T(4,128)(2,1)S(1)}, u32[]{:S(2)}, u32[]{:S(2)}) %all-to-all-start.2) | async-done | bytes 131104 | tf_op jit(solution)/shard_map/all_to_all | solution.py:210
  73.0 0.1 fusion.1
  73.0 0.2 reshape.49
  73.2 0.2 copy.29
  73.4 0.2 broadcast_in_dim.17
  73.6 0.8 broadcast_in_dim.18
  74.5 3.5 %all-to-all-start.3 = ((bf16[4,16,16,256]{3,2,1,0:T(8,128)(2,1)}), bf16[4,16,16,256]{3,2,1,0:T(8,128)(2,1)S(1)}, u32[]{:S(2)}, u32[]{:S(2)}) async-start(bf16[4,16,16,256]{3,2,1,0:T(8,128)(2,1)} %broadcast_in_dim.18), calls=%async_computation.3 | async-start | bytes 1048576 | tf_op jit(solution)/shard_map/all_to_all | solution.py:218
  78.0 6.9 %all-to-all-done.3.left_ref = bf16[4,16,16,256]{3,2,1,0:T(8,128)(2,1)S(1)} async-done(((bf16[4,16,16,256]{3,2,1,0:T(8,128)(2,1)}), bf16[4,16,16,256]{3,2,1,0:T(8,128)(2,1)S(1)}, u32[]{:S(2)}, u32[]{:S(2)}) %all-to-all-start.3) | async-done | bytes 524320 | tf_op jit(solution)/shard_map/all_to_all | solution.py:218
  84.9 0.2 turn.1.left_ref
  85.1 10.3 %all-gather.3.cloned.1.call-done = bf16[16384,128]{1,0:T(8,128)(2,1)} async-done(((bf16[1024,128]{1,0:T(8,128)(2,1)}), bf16[16384,128]{1,0:T(8,128)(2,1)}) %all-gather.3.cloned.1.call-update) | async-done | bytes 4194320 | tf_op jit(solution)/shard_map/all_gather | solution.py:200
  95.4 3.1 %project.1 = (bf16[4,4,64,256]{3,2,1,0:T(8,128)(2,1)S(1)}, bf16[4,4,64,256]{3,2,1,0:T(8,128)(2,1)S(1)}) custom-call(s32[1]{0:T(128)} %bitcast.me_ref, bf16[256,1024]{1,0:T(8,128)(2,1)S(1)} %turn.1.left_ref, bf16[16,1024,128]{2,1,0:T(8,128)(2,1)} %bitcast.33), custom_call_target="tpu_custom_call" | custom-call | flops 1073741824 | bytes 6000000 | tf_op jit(solution)/shard_map/project/pallas_call | solution.py:160
  98.5 10.5 %collective-permute-start = (bf16[4,4,64,256]{3,2,1,0:T(8,128)(2,1)S(1)}, bf16[4,4,64,256]{3,2,1,0:T(8,128)(2,1)S(1)}, u32[]{:S(2)}, u32[]{:S(2)}) collective-permute-start(bf16[4,4,64,256]{3,2,1,0:T(8,128)(2,1)S(1)} %get-tuple-element.8), channel_id=1, source_target_pairs={{0,1},{1,0},{2,3},{3,2},{4,5},{5,4},{6,7},{7,6},{8,9},{9,8},{10,11... | collective-permute-start | bytes 1572872 | tf_op jit(solution)/shard_map/ppermute | solution.py:222
  109.0 1.5 %collective-permute-done = bf16[4,4,64,256]{3,2,1,0:T(8,128)(2,1)S(1)} collective-permute-done((bf16[4,4,64,256]{3,2,1,0:T(8,128)(2,1)S(1)}, bf16[4,4,64,256]{3,2,1,0:T(8,128)(2,1)S(1)}, u32[]{:S(2)}, u32[]{:S(2)}) %collective-permute-start) | collective-permute-done | bytes 524320 | tf_op jit(solution)/shard_map/ppermute | solution.py:222
  110.5 0.2 add_convert_fusion
  110.7 16.4 %all_to_all.26 = bf16[16,64,256]{2,1,0:T(8,128)(2,1)S(1)} all-to-all(bf16[16,64,256]{2,1,0:T(8,128)(2,1)S(1)} %bitcast.34), channel_id=1, replica_groups=mesh['z'=16,'y'=4,'x'=4,'core'=2] {'y','x'}, dimensions={0} | all-to-all | bytes 1048576 | tf_op jit(solution)/shard_map/all_to_all | solution.py:225
  127.1 0.7 gather.1
  (6 shorter events, 0.2 us)
Async XLA Ops:
  6.5 42.2 %copy-start.3 = (bf16[256,128]{1,0:T(8,128)(2,1)S(1)}, bf16[256,128]{1,0:T(8,128)(2,1)}, u32[]{:S(2)}) copy-start(bf16[256,128]{1,0:T(8,128)(2,1)} %constant.23.clone.first_ref) | copy-start | bytes 196612
  6.5 42.2 %copy-start.1 = (f32[4,128,128]{2,1,0:T(8,128)S(1)}, f32[4,128,128]{2,1,0:T(8,128)}, u32[]{:S(2)}) copy-start(f32[4,128,128]{2,1,0:T(8,128)} %constant.24.clone.spin_ref) | copy-start | bytes 786436
  6.5 42.2 %copy-start = (bf16[2,384,256]{2,1,0:T(8,128)(2,1)S(1)}, bf16[2,384,256]{2,1,0:T(8,128)(2,1)}, u32[]{:S(2)}) copy-start(bf16[2,384,256]{2,1,0:T(8,128)(2,1)} %constant.25.clone.mid_ref) | copy-start | bytes 1179652
  6.5 42.2 %copy-start.2 = (bf16[128,384]{1,0:T(8,128)(2,1)S(1)}, bf16[128,384]{1,0:T(8,128)(2,1)}, u32[]{:S(2)}) copy-start(bf16[128,384]{1,0:T(8,128)(2,1)} %constant.26.clone.last_ref) | copy-start | bytes 294916
  6.5 29.5 %copy-start.4 = (f32[16,2,8192]{2,1,0:T(2,128)S(1)}, f32[16,2,8192]{2,1,0:T(2,128)}, u32[]{:S(2)}) copy-start(f32[16,2,8192]{2,1,0:T(2,128)} %param.11) | copy-start | bytes 3145732
  6.5 88.8 %all-gather.3.cloned.1.call-start = ((), (), s32[]{:S(2)}) async-start(), calls=%async_computation.5 | async-start | bytes 4456448 | tf_op jit(solution)/shard_map/all_gather | solution.py:200
  10.0 50.2 %copy-start.5 = (f32[1024]{0:T(1024)S(1)}, f32[1024]{0:T(1024)}, u32[]{:S(2)}) copy-start(f32[1024]{0:T(1024)} %param.12) | copy-start | bytes 12292
  21.1 27.6 %all-to-all-start.1 = ((bf16[16,4,1024]{2,1,0:T(4,128)(2,1)}), bf16[16,4,1024]{2,1,0:T(4,128)(2,1)S(1)}, u32[]{:S(2)}, u32[]{:S(2)}) async-start(bf16[16,4,1024]{2,1,0:T(4,128)(2,1)} %copy.27), calls=%async_computation.1 | async-start | bytes 262144 | tf_op jit(solution)/shard_map/all_to_all | solution.py:208
  54.2 18.8 %all-to-all-start.2 = ((bf16[16,4,1024]{2,1,0:T(4,128)(2,1)}), bf16[16,4,1024]{2,1,0:T(4,128)(2,1)S(1)}, u32[]{:S(2)}, u32[]{:S(2)}) async-start(bf16[16,4,1024]{2,1,0:T(4,128)(2,1)} %reshape.47), calls=%async_computation.2 | async-start | bytes 262144 | tf_op jit(solution)/shard_map/all_to_all | solution.py:210
  74.5 10.4 %all-to-all-start.3 = ((bf16[4,16,16,256]{3,2,1,0:T(8,128)(2,1)}), bf16[4,16,16,256]{3,2,1,0:T(8,128)(2,1)S(1)}, u32[]{:S(2)}, u32[]{:S(2)}) async-start(bf16[4,16,16,256]{3,2,1,0:T(8,128)(2,1)} %broadcast_in_dim.18), calls=%async_computation.3 | async-start | bytes 1048576 | tf_op jit(solution)/shard_map/all_to_all | solution.py:218
  98.5 12.1 %collective-permute-start = (bf16[4,4,64,256]{3,2,1,0:T(8,128)(2,1)S(1)}, bf16[4,4,64,256]{3,2,1,0:T(8,128)(2,1)S(1)}, u32[]{:S(2)}, u32[]{:S(2)}) collective-permute-start(bf16[4,4,64,256]{3,2,1,0:T(8,128)(2,1)S(1)} %get-tuple-element.8), channel_id=1, source_target_pairs={{0,1},{1,0},{2,3},{3,2},{4,5},{5,4},{6,7},{7,6},{8,9},{9,8},{10,11... | collective-permute-start | bytes 1572872 | tf_op jit(solution)/shard_map/ppermute | solution.py:222
Sparse Core Ops, SparseCore 0:
  9.5 85.8 all-gather.2

commit v3 on v2

--- a/solution.py
+++ b/solution.py
@@ -133,40 +133,40 @@
     )(left)
 
 
-def project_kernel(me_ref, left_ref, weight_ref, keep_ref, send_ref, held_ref, sems):
-    blocks, _, cols = weight_ref.shape
-    copies = [pltpu.make_async_copy(weight_ref.at[i], held_ref.at[i], sems.at[i]) for i in range(blocks)]
+def project_kernel(side_ref, left_ref, weight_ref, out_ref, held_ref, sems):
+    blocks, _, cols = held_ref.shape
+    pair = blocks // X
+    source = [(x * CORE + side_ref[0]) * pair + p for x in range(X) for p in range(pair)]
+    copies = [pltpu.make_async_copy(weight_ref.at[source[i]], held_ref.at[i], sems.at[i]) for i in range(blocks)]
     for copy in copies:
         copy.start()
     left = left_ref[...]
-    step = blocks // X
-    pair = step // CORE
-    mine = me_ref[0]
-    for x in range(X):
-        for p in range(step):
-            copies[x * step + p].wait()
-        order = [x * step + core * pair + p for core in (mine, 1 - mine) for p in range(pair)]
-        weight = jnp.concatenate([held_ref[i] for i in order], 1)
+    for x in range(0, X, 2):
+        for i in range(x * pair, (x + 2) * pair):
+            copies[i].wait()
+        weight = jnp.concatenate([held_ref[i] for i in range(x * pair, (x + 2) * pair)], 1)
         part = jnp.dot(left, weight, preferred_element_type=jnp.float32).astype(jnp.bfloat16)
-        keep_ref[:, x] = part[:, : pair * cols].reshape(keep_ref.shape[0], HALF, pair * cols)
-        send_ref[:, x] = part[:, pair * cols :].reshape(keep_ref.shape[0], HALF, pair * cols)
-
-
-def project(me, left, weight):
+        for k in range(2):
+            piece = part[:, k * pair * cols : (k + 1) * pair * cols]
+            out_ref[:, x + k] = piece.reshape(out_ref.shape[0], HALF, pair * cols)
+
+
+def project(side, left, weight, name):
     tokens, depth = left.shape
     blocks, _, cols = weight.shape
-    wide = blocks // (X * CORE) * cols
+    half = blocks // CORE
+    wide = half // X * cols
     vmem = pl.BlockSpec(memory_space=pltpu.VMEM)
     return pl.pallas_call(
         project_kernel,
-        out_shape=[jax.ShapeDtypeStruct((tokens // HALF, X, HALF, wide), jnp.bfloat16)] * 2,
+        out_shape=jax.ShapeDtypeStruct((tokens // HALF, X, HALF, wide), jnp.bfloat16),
         in_specs=[pl.BlockSpec(memory_space=pltpu.SMEM), vmem, pl.BlockSpec(memory_space=pl.ANY)],
-        out_specs=[vmem, vmem],
-        scratch_shapes=[pltpu.VMEM(weight.shape, weight.dtype), pltpu.SemaphoreType.DMA((blocks,))],
+        out_specs=vmem,
+        scratch_shapes=[pltpu.VMEM((half, depth, cols), weight.dtype), pltpu.SemaphoreType.DMA((half,))],
         compiler_params=pltpu.CompilerParams(vmem_limit_bytes=52 * 1024 * 1024),
-        cost_estimate=pl.CostEstimate(flops=2 * depth * tokens * blocks * cols, bytes_accessed=6_000_000, transcendentals=0),
-        name="project",
-    )(me, left, weight)
+        cost_estimate=pl.CostEstimate(flops=2 * depth * tokens * half * cols, bytes_accessed=3_000_000, transcendentals=0),
+        name=name,
+    )(side, left, weight)
 
 
 def gather_kernel(part_ref, out_ref):
@@ -218,8 +218,10 @@
     wide = lax.all_to_all(wide, "y", split_axis=0, concat_axis=0, tiled=True)
 
     me = lax.axis_index("core").astype(jnp.int32).reshape(1)
-    keep, send = project(me, turn(wide), weight)
+    left = turn(wide)
+    send = project(1 - me, left, weight, "project_send")
     other = lax.ppermute(send, "core", [(0, 1), (1, 0)])
+    keep = project(me, left, weight, "project_keep")
     part = (keep.astype(jnp.float32) + other.astype(jnp.float32)).astype(jnp.bfloat16)
     part = part.reshape((Y * X,) + part.shape[2:])
     part = lax.all_to_all(part, ("y", "x"), split_axis=0, concat_axis=0, tiled=True)

time: 135 us -> 135 us (level)
  waiting for transfers between devices: 43.6 us -> 42.1 us
    ppermute x1, waiting for transfers between devices: 1.51 us -> 0.01 us  [per_device(): other = lax.ppermute(send, 'core', [(0, 1), (1, 0)])]
    pallas_call x1 -> x2, Pallas kernels: 3.1 us -> 4.29 us  [project(): pl.pallas_call(project_kernel, out_shape=jax.ShapeDtypeStruct((tokens //...]
  transfers between devices with their start and end apart: 5 -> 5, of which waited for: 5 -> 4; matrix products, arithmetic and copies ran while one was open for 5% -> 5% of each run, Pallas kernels for 4% -> 5%
where the time goes in v3:
time: 135 us
  waiting for transfers between devices  42.1 us (31%)
  starting transfers between devices  35 us (26%)
  blocking collectives  27.1 us (20%)
  between operations  13.7 us (10%)
  Pallas kernels  9.88 us (7%)
  local copies, waits for them, and re-layouts  6.78 us (5%)
    all_to_all x1, blocking collectives, per_device(): lax.all_to_all(part, ('y', 'x'), split_axis=0, concat_axis=0, tiled=True)  16.8 us
    all_to_all x1, starting transfers between devices, per_device(): lax.all_to_all(sig.transpose(1, 0, 2), 'z', split_axis=0, concat_axis=0,...  14.9 us
    all_to_all x1, waiting for transfers between devices, per_device(): lax.all_to_all(conv.reshape(Z, Y, width * rows), 'z', split_axis=0, conca...  12.5 us
    all_to_all x1, waiting for transfers between devices, per_device(): lax.all_to_all(sig.transpose(1, 0, 2), 'z', split_axis=0, concat_axis=0,...  11.7 us
    ppermute x1, starting transfers between devices, per_device(): other = lax.ppermute(send, 'core', [(0, 1), (1, 0)])  10.5 us
    all_to_all x1, blocking collectives, per_device(): near = lax.all_to_all(near, 'y', split_axis=0, concat_axis=0, tiled=True)  10.3 us
    all_gather x1, waiting for transfers between devices, per_device(): weight = lax.all_gather(out_weight, 'z', axis=0, tiled=False)  10.3 us
    all_to_all x1, waiting for transfers between devices, per_device(): wide = lax.all_to_all(wide, 'y', split_axis=0, concat_axis=0, tiled=True)  6.94 us
  transfers between devices with their start and end apart: 5, of which 4 were waited for; matrix products, arithmetic and copies ran while one was open for 5% of the time, Pallas kernels for 5%

profile of v3, /device:TPU:1, one launch (start us, length us, event | category | flops | bytes accessed | tf_op | source)
XLA Modules:
  0.0 134.8 jit_solution(6663364515856389895)
XLA Ops:
  6.5 0.0 copy-start.3
  6.5 0.0 copy-start.1
  6.5 0.0 copy-start
  6.5 0.0 copy-start.2
  6.5 0.0 copy-start.4
  6.5 0.0 all-gather.3.cloned.1.call-start
  6.6 0.7 all-gather.3.cloned.1.call-update
  7.3 1.1 copy.23
  8.4 0.2 reshape.42
  8.6 1.1 copy.24
  9.7 0.2 reshape.44
  10.0 0.0 copy-start.5
  10.0 10.3 %all_to_all.25 = bf16[4,32,1024]{2,1,0:T(8,128)(2,1)S(1)} all-to-all(bf16[4,32,1024]{2,1,0:T(8,128)(2,1)S(1)} %pad_maximum_fusion), channel_id=1, replica_groups=mesh['z'=16,'y'=4,'x'=4,'core'=2] {'y'}, dimensions={0} | all-to-all | bytes 524288 | tf_op jit(solution)/shard_map/all_to_all | solution.py:206
  20.3 0.8 copy.27
  21.1 14.9 %all-to-all-start.1 = ((bf16[16,4,1024]{2,1,0:T(4,128)(2,1)}), bf16[16,4,1024]{2,1,0:T(4,128)(2,1)S(1)}, u32[]{:S(2)}, u32[]{:S(2)}) async-start(bf16[16,4,1024]{2,1,0:T(4,128)(2,1)} %copy.27), calls=%async_computation.1 | async-start | bytes 262144 | tf_op jit(solution)/shard_map/all_to_all | solution.py:208
  36.1 0.0 copy-done.4
  36.1 0.9 reshape.46.spec_ref
  37.0 11.7 %all-to-all-done.1 = bf16[16,4,1024]{2,1,0:T(4,128)(2,1)S(1)} async-done(((bf16[16,4,1024]{2,1,0:T(4,128)(2,1)}), bf16[16,4,1024]{2,1,0:T(4,128)(2,1)S(1)}, u32[]{:S(2)}, u32[]{:S(2)}) %all-to-all-start.1) | async-done | bytes 131104 | tf_op jit(solution)/shard_map/all_to_all | solution.py:208
  48.7 0.0 copy-done.3
  48.8 0.0 copy-done.1
  48.8 0.0 copy-done
  48.8 0.0 copy-done.2
  48.8 4.7 %long_conv.1 = bf16[64,1024]{1,0:T(8,128)(2,1)S(1)} custom-call(bf16[64,1024]{1,0:T(8,128)(2,1)S(1)} %reshape.45.sig_ref, f32[16,128,128]{2,1,0:T(8,128)S(1)} %reshape.46.spec_ref, bf16[256,128]{1,0:T(8,128)(2,1)S(1)} %copy-done.3, f32[4,128,128]{2,1,0:T(8,128)S(1)} %copy-done.1, bf16[2,384,256]{2,1,0:T(8,128)(2,1)S(1)} %copy-done, ...), custom_call_target="tpu_custom_call" | custom-call | flops 1200000000 | bytes 2000000 | tf_op jit(solution)/shard_map/long_conv/pallas_call | solution.py:106
  53.5 0.7 reshape.47
  54.2 6.0 %all-to-all-start.2 = ((bf16[16,4,1024]{2,1,0:T(4,128)(2,1)}), bf16[16,4,1024]{2,1,0:T(4,128)(2,1)S(1)}, u32[]{:S(2)}, u32[]{:S(2)}) async-start(bf16[16,4,1024]{2,1,0:T(4,128)(2,1)} %reshape.47), calls=%async_computation.2 | async-start | bytes 262144 | tf_op jit(solution)/shard_map/all_to_all | solution.py:210
  60.2 0.0 copy-done.5
  60.2 0.1 reshape.48
  60.3 0.1 broadcast_in_dim.16
  60.4 0.1 mul.13
  60.5 12.5 %all-to-all-done.2 = bf16[16,4,1024]{2,1,0:T(4,128)(2,1)S(1)} async-done(((bf16[16,4,1024]{2,1,0:T(4,128)(2,1)}), bf16[16,4,1024]{2,1,0:T(4,128)(2,1)S(1)}, u32[]{:S(2)}, u32[]{:S(2)}) %all-to-all-start.2) | async-done | bytes 131104 | tf_op jit(solution)/shard_map/all_to_all | solution.py:210
  73.0 0.1 fusion.1
  73.0 0.2 reshape.49
  73.2 0.2 copy.29
  73.4 0.2 broadcast_in_dim.17
  73.6 0.8 broadcast_in_dim.18
  74.5 3.5 %all-to-all-start.3 = ((bf16[4,16,16,256]{3,2,1,0:T(8,128)(2,1)}), bf16[4,16,16,256]{3,2,1,0:T(8,128)(2,1)S(1)}, u32[]{:S(2)}, u32[]{:S(2)}) async-start(bf16[4,16,16,256]{3,2,1,0:T(8,128)(2,1)} %broadcast_in_dim.18), calls=%async_computation.3 | async-start | bytes 1048576 | tf_op jit(solution)/shard_map/all_to_all | solution.py:218
  78.0 6.9 %all-to-all-done.3.left_ref = bf16[4,16,16,256]{3,2,1,0:T(8,128)(2,1)S(1)} async-done(((bf16[4,16,16,256]{3,2,1,0:T(8,128)(2,1)}), bf16[4,16,16,256]{3,2,1,0:T(8,128)(2,1)S(1)}, u32[]{:S(2)}, u32[]{:S(2)}) %all-to-all-start.3) | async-done | bytes 524320 | tf_op jit(solution)/shard_map/all_to_all | solution.py:218
  84.9 0.2 turn.1.left_ref
  85.1 10.3 %all-gather.3.cloned.1.call-done = bf16[16384,128]{1,0:T(8,128)(2,1)} async-done(((bf16[1024,128]{1,0:T(8,128)(2,1)}), bf16[16384,128]{1,0:T(8,128)(2,1)}) %all-gather.3.cloned.1.call-update) | async-done | bytes 4194320 | tf_op jit(solution)/shard_map/all_gather | solution.py:200
  95.4 2.1 %project_send.1 = bf16[4,4,64,256]{3,2,1,0:T(8,128)(2,1)S(1)} custom-call(s32[1]{0:T(128)S(6)} %sub.3.side_ref, bf16[256,1024]{1,0:T(8,128)(2,1)S(1)} %turn.1.left_ref, bf16[16,1024,128]{2,1,0:T(8,128)(2,1)} %bitcast.33), custom_call_target="tpu_custom_call" | custom-call | flops 536870912 | bytes 3000000 | tf_op jit(solution)/shard_map/project_send/pallas_call | solution.py:160
  97.5 10.5 %collective-permute-start = (bf16[4,4,64,256]{3,2,1,0:T(8,128)(2,1)S(1)}, bf16[4,4,64,256]{3,2,1,0:T(8,128)(2,1)S(1)}, u32[]{:S(2)}, u32[]{:S(2)}) collective-permute-start(bf16[4,4,64,256]{3,2,1,0:T(8,128)(2,1)S(1)} %project_send.1), channel_id=1, source_target_pairs={{0,1},{1,0},{2,3},{3,2},{4,5},{5,4},{6,7},{7,6},{8,9},{9,8},{10,11... | collective-permute-start | bytes 1572872 | tf_op jit(solution)/shard_map/ppermute | solution.py:223
  108.1 2.1 %project_keep.1 = bf16[4,4,64,256]{3,2,1,0:T(8,128)(2,1)S(1)} custom-call(s32[1]{0:T(128)} %bitcast.side_ref, bf16[256,1024]{1,0:T(8,128)(2,1)S(1)} %turn.1.left_ref, bf16[16,1024,128]{2,1,0:T(8,128)(2,1)} %bitcast.34), custom_call_target="tpu_custom_call" | custom-call | flops 536870912 | bytes 3000000 | tf_op jit(solution)/shard_map/project_keep/pallas_call | solution.py:160
  110.2 0.0 collective-permute-done
  110.2 0.2 add_convert_fusion
  110.4 16.8 %all_to_all.26 = bf16[16,64,256]{2,1,0:T(8,128)(2,1)S(1)} all-to-all(bf16[16,64,256]{2,1,0:T(8,128)(2,1)S(1)} %bitcast.35), channel_id=1, replica_groups=mesh['z'=16,'y'=4,'x'=4,'core'=2] {'y','x'}, dimensions={0} | all-to-all | bytes 1048576 | tf_op jit(solution)/shard_map/all_to_all | solution.py:227
  127.2 0.7 gather.1
  (6 shorter events, 0.2 us)
Async XLA Ops:
  6.5 42.2 %copy-start.3 = (bf16[256,128]{1,0:T(8,128)(2,1)S(1)}, bf16[256,128]{1,0:T(8,128)(2,1)}, u32[]{:S(2)}) copy-start(bf16[256,128]{1,0:T(8,128)(2,1)} %constant.25.clone.first_ref) | copy-start | bytes 196612
  6.5 42.2 %copy-start.1 = (f32[4,128,128]{2,1,0:T(8,128)S(1)}, f32[4,128,128]{2,1,0:T(8,128)}, u32[]{:S(2)}) copy-start(f32[4,128,128]{2,1,0:T(8,128)} %constant.26.clone.spin_ref) | copy-start | bytes 786436
  6.5 42.2 %copy-start = (bf16[2,384,256]{2,1,0:T(8,128)(2,1)S(1)}, bf16[2,384,256]{2,1,0:T(8,128)(2,1)}, u32[]{:S(2)}) copy-start(bf16[2,384,256]{2,1,0:T(8,128)(2,1)} %constant.27.clone.mid_ref) | copy-start | bytes 1179652
  6.5 42.2 %copy-start.2 = (bf16[128,384]{1,0:T(8,128)(2,1)S(1)}, bf16[128,384]{1,0:T(8,128)(2,1)}, u32[]{:S(2)}) copy-start(bf16[128,384]{1,0:T(8,128)(2,1)} %constant.28.clone.last_ref) | copy-start | bytes 294916
  6.5 29.5 %copy-start.4 = (f32[16,2,8192]{2,1,0:T(2,128)S(1)}, f32[16,2,8192]{2,1,0:T(2,128)}, u32[]{:S(2)}) copy-start(f32[16,2,8192]{2,1,0:T(2,128)} %param.11) | copy-start | bytes 3145732
  6.5 88.8 %all-gather.3.cloned.1.call-start = ((), (), s32[]{:S(2)}) async-start(), calls=%async_computation.5 | async-start | bytes 4456448 | tf_op jit(solution)/shard_map/all_gather | solution.py:200
  10.0 50.2 %copy-start.5 = (f32[1024]{0:T(1024)S(1)}, f32[1024]{0:T(1024)}, u32[]{:S(2)}) copy-start(f32[1024]{0:T(1024)} %param.12) | copy-start | bytes 12292
  21.1 27.6 %all-to-all-start.1 = ((bf16[16,4,1024]{2,1,0:T(4,128)(2,1)}), bf16[16,4,1024]{2,1,0:T(4,128)(2,1)S(1)}, u32[]{:S(2)}, u32[]{:S(2)}) async-start(bf16[16,4,1024]{2,1,0:T(4,128)(2,1)} %copy.27), calls=%async_computation.1 | async-start | bytes 262144 | tf_op jit(solution)/shard_map/all_to_all | solution.py:208
  54.2 18.8 %all-to-all-start.2 = ((bf16[16,4,1024]{2,1,0:T(4,128)(2,1)}), bf16[16,4,1024]{2,1,0:T(4,128)(2,1)S(1)}, u32[]{:S(2)}, u32[]{:S(2)}) async-start(bf16[16,4,1024]{2,1,0:T(4,128)(2,1)} %reshape.47), calls=%async_computation.2 | async-start | bytes 262144 | tf_op jit(solution)/shard_map/all_to_all | solution.py:210
  74.5 10.4 %all-to-all-start.3 = ((bf16[4,16,16,256]{3,2,1,0:T(8,128)(2,1)}), bf16[4,16,16,256]{3,2,1,0:T(8,128)(2,1)S(1)}, u32[]{:S(2)}, u32[]{:S(2)}) async-start(bf16[4,16,16,256]{3,2,1,0:T(8,128)(2,1)} %broadcast_in_dim.18), calls=%async_computation.3 | async-start | bytes 1048576 | tf_op jit(solution)/shard_map/all_to_all | solution.py:218
  97.5 12.7 %collective-permute-start = (bf16[4,4,64,256]{3,2,1,0:T(8,128)(2,1)S(1)}, bf16[4,4,64,256]{3,2,1,0:T(8,128)(2,1)S(1)}, u32[]{:S(2)}, u32[]{:S(2)}) collective-permute-start(bf16[4,4,64,256]{3,2,1,0:T(8,128)(2,1)S(1)} %project_send.1), channel_id=1, source_target_pairs={{0,1},{1,0},{2,3},{3,2},{4,5},{5,4},{6,7},{7,6},{8,9},{9,8},{10,11... | collective-permute-start | bytes 1572872 | tf_op jit(solution)/shard_map/ppermute | solution.py:223
Sparse Core Ops, SparseCore 0:
  9.5 85.8 all-gather.2

commit v4 on v2

v4 whole, which is shorter than its diff:
```python
import jax
import jax.numpy as jnp
import numpy as np
from jax import lax
from jax.experimental import pallas as pl
from jax.experimental.pallas import tpu as pltpu
from jax.sharding import Mesh, PartitionSpec as P

ZH, ZL, Y, X, CORE = 8, 2, 4, 4, 2
NEAR = ZL * Y
HALF = 64
TALL = 128
FFT = 8192


def split(table):
    top = table.astype(jnp.bfloat16)
    rest = (table - top.astype(np.float64)).astype(jnp.bfloat16)
    return top, rest


def fft_tables():
    turn = 2.0 * np.pi
    k, s, m = np.arange(TALL), np.arange(HALF), np.arange(HALF)
    one = turn * (np.outer(k, s) % TALL) / TALL
    first = np.concatenate([np.cos(one), np.sin(one)], 0)
    first = np.concatenate(split(first), 1)
    spin = turn * np.outer(k, m) / FFT
    cos, sin = np.cos(spin), np.sin(spin)
    fwd = np.stack([np.concatenate([cos, -sin], 1), np.concatenate([-sin, -cos], 1)])
    inv = np.stack([np.concatenate([cos, cos], 1), np.concatenate([-sin, sin], 1)])
    two = turn * (np.outer(m, m) % HALF) / HALF
    c2, s2 = np.cos(two), np.sin(two)
    ahead = np.block([[c2, -s2, -s2, c2], [s2, c2, c2, s2]])
    back = np.block([[c2, s2, s2, c2], [-s2, c2, c2, -s2]])

    def triple(table):
        top, rest = split(table)
        return np.concatenate([top, top, rest], 0)

    four = turn * (np.outer(s, k) % TALL) / TALL
    last = np.concatenate([np.cos(four), -np.sin(four)], 0) / FFT
    top, rest = split(last)
    last = np.concatenate([top, top, rest], 1)
    return (
        first,
        np.concatenate([fwd, inv]).astype(np.float32),
        np.stack([triple(ahead), triple(back)]),
        last,
    )


def pieces(value):
    top = value.astype(jnp.bfloat16)
    rest = (value - top.astype(jnp.float32)).astype(jnp.bfloat16)
    return [top, rest, top]


GANG = 4


def conv_kernel(both_ref, spec_ref, skip_ref, first_ref, spin_ref, mid_ref, last_ref, out_ref):
    width = 2 * HALF
    left = lax.broadcasted_iota(jnp.int32, (1, width), 1) < HALF
    fp, fq, ip, iq = [spin_ref[i] for i in range(4)]

    def swap(value):
        return pltpu.roll(value, HALF, 1)

    def dot(one, two):
        return jnp.dot(one, two, preferred_element_type=jnp.float32)

    for start in range(0, both_ref.shape[0], GANG):
        gang = range(GANG)
        data = [both_ref[start + c].astype(jnp.float32) for c in gang]
        other = [swap(data[c]) for c in gang]
        wide = jnp.concatenate([jnp.where(left, data[c], other[c]) for c in gang], 1).astype(jnp.bfloat16)
        both = dot(first_ref[...], jnp.concatenate([wide, wide], 0))
        at = [slice(c * width, (c + 1) * width) for c in gang]
        tall = [slice(c * TALL, (c + 1) * TALL) for c in gang]
        turned = jnp.concatenate([both[:TALL, at[c]] * fp + both[TALL:, at[c]] * fq for c in gang], 0)
        freq = dot(jnp.concatenate(pieces(turned), 1), mid_ref[0])
        filt = jnp.concatenate([spec_ref[start + c].T for c in gang], 0)
        turned_filt = swap(filt)
        prod = freq[:, :width] * jnp.where(left, filt, turned_filt) + freq[:, width:] * jnp.where(
            left, -turned_filt, filt
        )
        back = dot(jnp.concatenate(pieces(prod), 1), mid_ref[1])
        spun = jnp.concatenate([back[tall[c], :width] * ip + back[tall[c], width:] * iq for c in gang], 1)
        ends = dot(last_ref[...], jnp.concatenate(pieces(spun), 0))
        for c in range(0, GANG, 2):
            even, odd = ends[:, at[c]], ends[:, at[c + 1]]
            conv = jnp.where(left, even[:HALF], odd[HALF:]) + swap(jnp.where(left, odd[:HALF], even[HALF:]))
            conv = conv.astype(jnp.bfloat16).astype(jnp.float32)
            value = jnp.where(left, data[c], other[c + 1])
            gate = jnp.where(left, other[c], data[c + 1])
            lanes = slice((start + c) * HALF, (start + c + 2) * HALF)
            out_ref[:, lanes] = (gate * (conv + skip_ref[:, lanes] * value)).astype(jnp.bfloat16)


def gated_conv(both, spec, skip):
    width, length, lanes = both.shape
    tables = fft_tables()
    vmem = pl.BlockSpec(memory_space=pltpu.VMEM)
    return pl.pallas_call(
        conv_kernel,
        out_shape=jax.ShapeDtypeStruct((length, width * lanes // 2), jnp.bfloat16),
        in_specs=[vmem] * 7,
        out_specs=vmem,
        compiler_params=pltpu.CompilerParams(vmem_limit_bytes=32 * 1024 * 1024),
        cost_estimate=pl.CostEstimate(flops=1_200_000_000, bytes_accessed=2_000_000, transcendentals=0),
        name="gated_conv",
    )(both, spec, skip, *[jnp.asarray(t) for t in tables])


def spread_kernel(left_ref, out_ref):
    for spot in range(out_ref.shape[0]):
        out_ref[spot] = left_ref[...]


def spread(left):
    vmem = pl.BlockSpec(memory_space=pltpu.VMEM)
    return pl.pallas_call(
        spread_kernel,
        out_shape=jax.ShapeDtypeStruct((NEAR,) + left.shape, jnp.bfloat16),
        in_specs=[vmem],
        out_specs=vmem,
        compiler_params=pltpu.CompilerParams(vmem_limit_bytes=32 * 1024 * 1024),
        name="spread",
    )(left)


def turn_kernel(left_ref, out_ref):
    near, far = left_ref.shape[:2]
    blocks = [left_ref[a, b] for b in range(far) for a in range(near)]
    out_ref[...] = jnp.concatenate(blocks, 0).T


def turn(left):
    near, far, width, tokens = left.shape
    vmem = pl.BlockSpec(memory_space=pltpu.VMEM)
    return pl.pallas_call(
        turn_kernel,
        out_shape=jax.ShapeDtypeStruct((tokens, near * far * width), jnp.bfloat16),
        in_specs=[vmem],
        out_specs=vmem,
        compiler_params=pltpu.CompilerParams(vmem_limit_bytes=32 * 1024 * 1024),
        name="turn",
    )(left)


def project_kernel(me_ref, left_ref, weight_ref, keep_ref, send_ref, held_ref, sems):
    blocks, _, cols = held_ref.shape
    copies = [pltpu.make_async_copy(weight_ref.at[i], held_ref.at[i], sems.at[i]) for i in range(blocks)]
    for copy in copies:
        copy.start()
    left = left_ref[...]
    mine = me_ref[0]
    for x in range(0, X, 2):
        for i in range(x * CORE, (x + 2) * CORE):
            copies[i].wait()
        order = [(x + k) * CORE + core for core in (mine, 1 - mine) for k in range(2)]
        weight = jnp.concatenate([held_ref[i] for i in order], 1)
        part = jnp.dot(left, weight, preferred_element_type=jnp.float32).astype(jnp.bfloat16)
        for k in range(2):
            for to_ref, at in ((keep_ref, k), (send_ref, 2 + k)):
                to_ref[:, x + k] = part[:, at * cols : (at + 1) * cols].reshape(to_ref.shape[0], HALF, cols)


def project(me, left, weight):
    tokens, depth = left.shape
    blocks, _, cols = weight.shape
    vmem = pl.BlockSpec(memory_space=pltpu.VMEM)
    return pl.pallas_call(
        project_kernel,
        out_shape=[jax.ShapeDtypeStruct((tokens // HALF, X, HALF, cols), jnp.bfloat16)] * 2,
        in_specs=[pl.BlockSpec(memory_space=pltpu.SMEM), vmem, pl.BlockSpec(memory_space=pl.ANY)],
        out_specs=[vmem, vmem],
        scratch_shapes=[pltpu.VMEM(weight.shape, weight.dtype), pltpu.SemaphoreType.DMA((blocks,))],
        compiler_params=pltpu.CompilerParams(vmem_limit_bytes=52 * 1024 * 1024),
        cost_estimate=pl.CostEstimate(flops=2 * depth * tokens * blocks * cols, bytes_accessed=4_000_000, transcendentals=0),
        name="project",
    )(me, left, weight)


def pair_kernel(values_ref, gate_ref, out_ref, held_ref, sems):
    copies = [pltpu.make_async_copy(ref, held_ref.at[i], sems.at[i]) for i, ref in enumerate((values_ref, gate_ref))]
    for copy in copies:
        copy.start()
    for copy in copies:
        copy.wait()
    out_ref[...] = jnp.concatenate([held_ref[0], held_ref[1]], 0).T


def pair(values, gate):
    rows, group = values.shape
    away = pl.BlockSpec(memory_space=pl.ANY)
    return pl.pallas_call(
        pair_kernel,
        out_shape=jax.ShapeDtypeStruct((group, 2 * rows), jnp.bfloat16),
        in_specs=[away, away],
        out_specs=pl.BlockSpec(memory_space=pltpu.VMEM),
        scratch_shapes=[pltpu.VMEM((2, rows, group), jnp.bfloat16), pltpu.SemaphoreType.DMA((2,))],
        compiler_params=pltpu.CompilerParams(vmem_limit_bytes=56 * 1024 * 1024),
        name="pair",
    )(values, gate)


def per_device(values, gate, spectrum, bias, out_weight):
    rows, group = values.shape
    width = group // (ZH * NEAR)
    cols = out_weight.shape[1]
    weight = lax.all_gather(out_weight, "zh", axis=0, tiled=False)

    nseq = ZH * NEAR
    both = pair(values, gate).reshape(nseq, width, 2 * rows)
    both = lax.all_to_all(both, ("zh", "zl", "y"), split_axis=0, concat_axis=0, tiled=True)
    seq = lax.axis_index(("zh", "zl", "y"))
    skip = lax.dynamic_slice(bias, (seq * width,), (width,))
    skip = jnp.broadcast_to(skip[:, None], (width, rows)).reshape(1, width * rows)
    gated = gated_conv(both.transpose(1, 0, 2), spectrum.reshape(width, TALL, TALL), skip)

    gated = gated.reshape(ZH, NEAR, width * rows)
    gated = lax.all_to_all(gated, "zh", split_axis=0, concat_axis=0, tiled=True)
    left = gated.reshape(ZH, NEAR, width, rows).transpose(0, 2, 1, 3).reshape(ZH, width, NEAR * rows)

    def there(block):
        wide = jnp.broadcast_to(block[None], (NEAR,) + block.shape)
        return turn(lax.all_to_all(wide, ("zl", "y"), split_axis=0, concat_axis=0, tiled=True))

    def again(block):
        wide = lax.all_to_all(spread(block), ("zl", "y"), split_axis=0, concat_axis=0, tiled=True)
        return wide.transpose(3, 1, 0, 2).reshape(NEAR * rows, group)

    left = lax.cond(bias[0] < 1e9, there, again, left)
    me = lax.axis_index("core").astype(jnp.int32).reshape(1)
    keep, send = project(me, left, weight)
    other = lax.ppermute(send, "core", [(0, 1), (1, 0)])
    part = (keep.astype(jnp.float32) + other.astype(jnp.float32)).astype(jnp.bfloat16)
    part = part.reshape((NEAR * X,) + part.shape[2:])
    part = lax.all_to_all(part, ("zl", "y", "x"), split_axis=0, concat_axis=0, tiled=True)
    total = jnp.sum(part.reshape(NEAR, X, rows, cols).astype(jnp.float32), axis=1).astype(jnp.bfloat16)
    return total.transpose(1, 0, 2).reshape(rows, -1)


def solution(mesh):
    names = ("zh", "zl", "y", "x", "core")
    fine = Mesh(mesh.devices.reshape(ZH, ZL, Y, X, CORE), names)
    seq, chan = names[:3], names[3:]
    placed = (
        P(seq, chan),
        P(seq, chan),
        P(chan + seq, None, None),
        P(chan),
        P(chan, seq),
    )
    return jax.shard_map(
        per_device, mesh=fine, in_specs=placed, out_specs=P(seq, chan), check_vma=False
    )
```

time: 135 us -> 132 us (0.978)
  blocking collectives: 26.8 us -> 34.5 us
  waiting for transfers between devices: 43.6 us -> 37.9 us
  starting transfers between devices: 35 us -> 30.2 us
    all_gather x1, waiting for transfers between devices: 10.3 us -> 0.02 us  [per_device(): weight = lax.all_gather(out_weight, 'zh', axis=0, tiled=False)]
    all_to_all x2, blocking collectives: 26.8 us -> 34.5 us  [the longest x1 19.4 us: there(): lax.all_to_all(wide, ('zl', 'y'), split_axis=0, concat_axis=0, tiled=True)]
    ppermute x1, starting transfers between devices: 10.5 us -> 5.7 us  [per_device(): other = lax.ppermute(send, 'core', [(0, 1), (1, 0)])]
    all_to_all x3 -> x2, waiting for transfers between devices: 31.1 us -> 35.7 us  [the longest x1 19 us: per_device(): lax.all_to_all(both, ('zh', 'zl', 'y'), split_axis=0, concat_axis=0, tile...]
    unnamed x14 -> x8, local copies, waits for them, and re-layouts: 2.17 us -> 0.01 us
    all_to_all x3 -> x2, starting transfers between devices: 24.4 us -> 24.5 us  [the longest x1 19.3 us: per_device(): lax.all_to_all(both, ('zh', 'zl', 'y'), split_axis=0, concat_axis=0, tile...]
  transfers between devices with their start and end apart: 5 -> 4, of which waited for: 5 -> 3; matrix products, arithmetic and copies ran while one was open for 5% -> 4% of each run, Pallas kernels for 4% -> 5%
where the time goes in v4:
time: 132 us
  waiting for transfers between devices  37.9 us (29%)
  blocking collectives  34.5 us (26%)
  starting transfers between devices  30.2 us (23%)
  between operations  14.2 us (11%)
  Pallas kernels  9.18 us (7%)
  local copies, waits for them, and re-layouts  5.63 us (4%)
    all_to_all x1, blocking collectives, there(): lax.all_to_all(wide, ('zl', 'y'), split_axis=0, concat_axis=0, tiled=True)  19.4 us
    all_to_all x1, starting transfers between devices, per_device(): lax.all_to_all(both, ('zh', 'zl', 'y'), split_axis=0, concat_axis=0, tile...  19.3 us
    all_to_all x1, waiting for transfers between devices, per_device(): lax.all_to_all(both, ('zh', 'zl', 'y'), split_axis=0, concat_axis=0, tile...  19 us
    all_to_all x1, waiting for transfers between devices, per_device(): gated = lax.all_to_all(gated, 'zh', split_axis=0, concat_axis=0, tiled=True)  16.7 us
    all_to_all x1, blocking collectives, per_device(): lax.all_to_all(part, ('zl', 'y', 'x'), split_axis=0, concat_axis=0, tiled...  15.1 us
    ppermute x1, starting transfers between devices, per_device(): other = lax.ppermute(send, 'core', [(0, 1), (1, 0)])  5.7 us
    all_to_all x1, starting transfers between devices, per_device(): gated = lax.all_to_all(gated, 'zh', split_axis=0, concat_axis=0, tiled=True)  5.22 us
    pallas_call x1, Pallas kernels, gated_conv(): pl.pallas_call(conv_kernel, out_shape=jax.ShapeDtypeStruct((length, width...  4.34 us
  transfers between devices with their start and end apart: 4, of which 3 were waited for; matrix products, arithmetic and copies ran while one was open for 4% of the time, Pallas kernels for 5%

profile of v4, /device:TPU:1, one launch (start us, length us, event | category | flops | bytes accessed | tf_op | source)
XLA Modules:
  0.0 132.0 jit_solution(16065452078227275638)
XLA Ops:
  6.5 0.0 copy-start.3
  6.5 0.0 copy-start.1
  6.5 0.0 copy-start
  6.5 0.0 copy-start.2
  6.5 0.0 all-gather.3.cloned.1.call-start
  6.6 0.7 all-gather.3.cloned.1.call-update
  7.3 1.8 %pair.1 = bf16[1024,128]{1,0:T(8,128)(2,1)} custom-call(bf16[64,1024]{1,0:T(8,128)(2,1)} %values_ref.1, bf16[64,1024]{1,0:T(8,128)(2,1)} %gate_ref.1), custom_call_target="tpu_custom_call" | custom-call | tf_op jit(solution)/shard_map/pair/pallas_call | solution.py:198
  9.1 19.3 %all-to-all-start.2 = ((bf16[64,16,128]{2,1,0:T(8,128)(2,1)}), bf16[64,16,128]{2,1,0:T(8,128)(2,1)S(1)}, u32[]{:S(2)}, u32[]{:S(2)}) async-start(bf16[64,16,128]{2,1,0:T(8,128)(2,1)} %bitcast.30), calls=%async_computation.2 | async-start | bytes 524288 | tf_op jit(solution)/shard_map/all_to_all | solution.py:217
  28.4 0.8 dynamic_slice.3
  29.2 0.1 broadcast_in_dim.6
  29.2 0.1 reshape.45.skip_ref
  29.3 2.1 %reshape.44.spec_ref = f32[16,128,128]{2,1,0:T(8,128)S(1)} reshape(f32[16,2,8192]{2,1,0:T(2,128)} %param.13) | data formatting | bytes 2097152 | tf_op jit(solution)/shard_map/reshape | solution.py:221
  31.4 19.0 %all-to-all-done.2 = bf16[64,16,128]{2,1,0:T(8,128)(2,1)S(1)} async-done(((bf16[64,16,128]{2,1,0:T(8,128)(2,1)}), bf16[64,16,128]{2,1,0:T(8,128)(2,1)S(1)}, u32[]{:S(2)}, u32[]{:S(2)}) %all-to-all-start.2) | async-done | bytes 262176 | tf_op jit(solution)/shard_map/all_to_all | solution.py:217
  50.5 0.1 copy.34
  50.6 0.0 copy-done.3
  50.6 0.0 copy-done.1
  50.6 0.0 copy-done
  50.6 0.0 copy-done.2
  50.6 4.3 %gated_conv.1 = bf16[64,1024]{1,0:T(8,128)(2,1)} custom-call(bf16[16,64,128]{2,1,0:T(8,128)(2,1)S(1)} %bitcast.24, f32[16,128,128]{2,1,0:T(8,128)S(1)} %reshape.44.spec_ref, f32[1,1024]{1,0:T(1,128)S(1)} %reshape.45.skip_ref, bf16[256,128]{1,0:T(8,128)(2,1)S(1)} %copy-done.3, f32[4,128,128]{2,1,0:T(8,128)S(1)} %copy-done.1, ...), custom_call_target="tpu_custom_call" | custom-call | flops 1200000000 | bytes 2000000 | tf_op jit(solution)/shard_map/gated_conv/pallas_call | solution.py:105
  54.9 5.2 %all-to-all-start.3 = ((bf16[8,8,1024]{2,1,0:T(8,128)(2,1)}), bf16[8,8,1024]{2,1,0:T(8,128)(2,1)S(1)}, u32[]{:S(2)}, u32[]{:S(2)}) async-start(bf16[8,8,1024]{2,1,0:T(8,128)(2,1)} %bitcast.6), calls=%async_computation.3 | async-start | bytes 262144 | tf_op jit(solution)/shard_map/all_to_all | solution.py:224
  60.2 1.3 slice.3
  62.1 16.7 %all-to-all-done.3 = bf16[8,8,1024]{2,1,0:T(8,128)(2,1)S(1)} async-done(((bf16[8,8,1024]{2,1,0:T(8,128)(2,1)}), bf16[8,8,1024]{2,1,0:T(8,128)(2,1)S(1)}, u32[]{:S(2)}, u32[]{:S(2)}) %all-to-all-start.3) | async-done | bytes 131104 | tf_op jit(solution)/shard_map/all_to_all | solution.py:224
  78.8 0.2 reshape.47
  79.0 20.1 %conditional.1 = (bf16[512,1024]{1,0:T(8,128)(2,1)S(1)}) conditional(s32[]{:T(128)} %bitcast.3, bf16[8,16,8,64]{3,1,2,0:T(8,128)(2,1)S(1)} %bitcast.27, bf16[8,16,8,64]{3,1,2,0:T(8,128)(2,1)S(1)} %bitcast.28), branch_computations={%region_0.0_spmd, %region_1.0_spmd} | conditional | bytes 6815752 | solution.py:235
  79.0 0.1 copy.26
  79.1 0.2 broadcast_in_dim.0
  79.3 0.1 broadcast_in_dim.1
  79.4 19.4 %all_to_all.24.left_ref = bf16[8,8,16,512]{3,2,1,0:T(8,128)(2,1)S(1)} all-to-all(bf16[8,8,16,512]{3,2,1,0:T(8,128)(2,1)S(1)} %broadcast_in_dim.1), channel_id=1, replica_groups=mesh['zh'=8,'zl'=2,'y'=4,'x'=4,'core'=2] {'zl','y'}, dimensions={0} | all-to-all | bytes 2097152 | tf_op jit(solution)/shard_map/cond/branch_1_fun/all_to_all | solution.py:229
  98.8 0.3 turn.1
  99.1 0.0 all-gather.3.cloned.1.call-done
  99.1 2.7 %project.1 = (bf16[8,4,64,128]{3,2,1,0:T(8,128)(2,1)S(1)}, bf16[8,4,64,128]{3,2,1,0:T(8,128)(2,1)S(1)}) custom-call(s32[1]{0:T(128)} %bitcast.2.me_ref, bf16[512,1024]{1,0:T(8,128)(2,1)S(1)} %get-tuple-element.15.left_ref, bf16[8,1024,128]{2,1,0:T(8,128)(2,1)} %bitcast.31), custom_call_target="tpu_custom_call" | custom-call | flops 1073741824 | bytes 4000000 | tf_op jit(solution)/shard_map/project/pallas_call | solution.py:174
  101.8 5.7 %collective-permute-start = (bf16[8,4,64,128]{3,2,1,0:T(8,128)(2,1)S(1)}, bf16[8,4,64,128]{3,2,1,0:T(8,128)(2,1)S(1)}, u32[]{:S(2)}, u32[]{:S(2)}) collective-permute-start(bf16[8,4,64,128]{3,2,1,0:T(8,128)(2,1)S(1)} %get-tuple-element.14), channel_id=1, source_target_pairs={{0,1},{1,0},{2,3},{3,2},{4,5},{5,4},{6,7},{7,6},{8,9},{9,8},{10,11... | collective-permute-start | bytes 1572872 | tf_op jit(solution)/shard_map/ppermute | solution.py:238
  107.5 1.5 %collective-permute-done = bf16[8,4,64,128]{3,2,1,0:T(8,128)(2,1)S(1)} collective-permute-done((bf16[8,4,64,128]{3,2,1,0:T(8,128)(2,1)S(1)}, bf16[8,4,64,128]{3,2,1,0:T(8,128)(2,1)S(1)}, u32[]{:S(2)}, u32[]{:S(2)}) %collective-permute-start) | collective-permute-done | bytes 524320 | tf_op jit(solution)/shard_map/ppermute | solution.py:238
  109.1 0.2 add_convert_fusion
  109.2 15.1 %all_to_all.25 = bf16[32,64,128]{2,1,0:T(8,128)(2,1)S(1)} all-to-all(bf16[32,64,128]{2,1,0:T(8,128)(2,1)S(1)} %bitcast.29), channel_id=1, replica_groups=mesh['zh'=8,'zl'=2,'y'=4,'x'=4,'core'=2] {'zl','y','x'}, dimensions={0} | all-to-all | bytes 1048576 | tf_op jit(solution)/shard_map/all_to_all | solution.py:241
  124.4 0.1 bitcast_reduce_fusion
  124.4 0.7 copy_bitcast_fusion.1
Async XLA Ops:
  6.5 44.0 %copy-start.3 = (bf16[256,128]{1,0:T(8,128)(2,1)S(1)}, bf16[256,128]{1,0:T(8,128)(2,1)}, u32[]{:S(2)}) copy-start(bf16[256,128]{1,0:T(8,128)(2,1)} %constant.42.clone.first_ref) | copy-start | bytes 196612
  6.5 44.0 %copy-start.1 = (f32[4,128,128]{2,1,0:T(8,128)S(1)}, f32[4,128,128]{2,1,0:T(8,128)}, u32[]{:S(2)}) copy-start(f32[4,128,128]{2,1,0:T(8,128)} %constant.43.clone.spin_ref) | copy-start | bytes 786436
  6.5 44.0 %copy-start = (bf16[2,384,256]{2,1,0:T(8,128)(2,1)S(1)}, bf16[2,384,256]{2,1,0:T(8,128)(2,1)}, u32[]{:S(2)}) copy-start(bf16[2,384,256]{2,1,0:T(8,128)(2,1)} %constant.44.clone.mid_ref) | copy-start | bytes 1179652
  6.5 44.1 %copy-start.2 = (bf16[128,384]{1,0:T(8,128)(2,1)S(1)}, bf16[128,384]{1,0:T(8,128)(2,1)}, u32[]{:S(2)}) copy-start(bf16[128,384]{1,0:T(8,128)(2,1)} %constant.45.clone.last_ref) | copy-start | bytes 294916
  6.5 92.6 %all-gather.3.cloned.1.call-start = ((), (), s32[]{:S(2)}) async-start(), calls=%async_computation.5 | async-start | bytes 2359296 | tf_op jit(solution)/shard_map/all_gather | solution.py:213
  9.1 41.4 %all-to-all-start.2 = ((bf16[64,16,128]{2,1,0:T(8,128)(2,1)}), bf16[64,16,128]{2,1,0:T(8,128)(2,1)S(1)}, u32[]{:S(2)}, u32[]{:S(2)}) async-start(bf16[64,16,128]{2,1,0:T(8,128)(2,1)} %bitcast.30), calls=%async_computation.2 | async-start | bytes 524288 | tf_op jit(solution)/shard_map/all_to_all | solution.py:217
  54.9 23.8 %all-to-all-start.3 = ((bf16[8,8,1024]{2,1,0:T(8,128)(2,1)}), bf16[8,8,1024]{2,1,0:T(8,128)(2,1)S(1)}, u32[]{:S(2)}, u32[]{:S(2)}) async-start(bf16[8,8,1024]{2,1,0:T(8,128)(2,1)} %bitcast.6), calls=%async_computation.3 | async-start | bytes 262144 | tf_op jit(solution)/shard_map/all_to_all | solution.py:224
  101.8 7.2 %collective-permute-start = (bf16[8,4,64,128]{3,2,1,0:T(8,128)(2,1)S(1)}, bf16[8,4,64,128]{3,2,1,0:T(8,128)(2,1)S(1)}, u32[]{:S(2)}, u32[]{:S(2)}) collective-permute-start(bf16[8,4,64,128]{3,2,1,0:T(8,128)(2,1)S(1)} %get-tuple-element.14), channel_id=1, source_target_pairs={{0,1},{1,0},{2,3},{3,2},{4,5},{5,4},{6,7},{7,6},{8,9},{9,8},{10,11... | collective-permute-start | bytes 1572872 | tf_op jit(solution)/shard_map/ppermute | solution.py:238
Sparse Core Ops, SparseCore 0:
  9.5 84.7 all-gather.2

commit v5 on v4

--- a/solution.py
+++ b/solution.py
@@ -56,7 +56,7 @@
     return [top, rest, top]
 
 
-GANG = 4
+GANG = 8
 
 
 def conv_kernel(both_ref, spec_ref, skip_ref, first_ref, spin_ref, mid_ref, last_ref, out_ref):
@@ -149,38 +149,36 @@
     )(left)
 
 
-def project_kernel(me_ref, left_ref, weight_ref, keep_ref, send_ref, held_ref, sems):
+def project_kernel(side_ref, left_ref, weight_ref, out_ref, held_ref, sems):
     blocks, _, cols = held_ref.shape
-    copies = [pltpu.make_async_copy(weight_ref.at[i], held_ref.at[i], sems.at[i]) for i in range(blocks)]
+    copies = [
+        pltpu.make_async_copy(weight_ref.at[x * CORE + side_ref[0]], held_ref.at[x], sems.at[x]) for x in range(blocks)
+    ]
     for copy in copies:
         copy.start()
-    left = left_ref[...]
-    mine = me_ref[0]
-    for x in range(0, X, 2):
-        for i in range(x * CORE, (x + 2) * CORE):
-            copies[i].wait()
-        order = [(x + k) * CORE + core for core in (mine, 1 - mine) for k in range(2)]
-        weight = jnp.concatenate([held_ref[i] for i in order], 1)
-        part = jnp.dot(left, weight, preferred_element_type=jnp.float32).astype(jnp.bfloat16)
-        for k in range(2):
-            for to_ref, at in ((keep_ref, k), (send_ref, 2 + k)):
-                to_ref[:, x + k] = part[:, at * cols : (at + 1) * cols].reshape(to_ref.shape[0], HALF, cols)
-
-
-def project(me, left, weight):
+    for copy in copies:
+        copy.wait()
+    weight = jnp.concatenate([held_ref[x] for x in range(blocks)], 1)
+    part = jnp.dot(left_ref[...], weight, preferred_element_type=jnp.float32).astype(jnp.bfloat16)
+    for x in range(blocks):
+        out_ref[:, x] = part[:, x * cols : (x + 1) * cols].reshape(out_ref.shape[0], HALF, cols)
+
+
+def project(side, left, weight, name):
     tokens, depth = left.shape
     blocks, _, cols = weight.shape
+    half = blocks // CORE
     vmem = pl.BlockSpec(memory_space=pltpu.VMEM)
     return pl.pallas_call(
         project_kernel,
-        out_shape=[jax.ShapeDtypeStruct((tokens // HALF, X, HALF, cols), jnp.bfloat16)] * 2,
+        out_shape=jax.ShapeDtypeStruct((tokens // HALF, X, HALF, cols), jnp.bfloat16),
         in_specs=[pl.BlockSpec(memory_space=pltpu.SMEM), vmem, pl.BlockSpec(memory_space=pl.ANY)],
-        out_specs=[vmem, vmem],
-        scratch_shapes=[pltpu.VMEM(weight.shape, weight.dtype), pltpu.SemaphoreType.DMA((blocks,))],
+        out_specs=vmem,
+        scratch_shapes=[pltpu.VMEM((half, depth, cols), weight.dtype), pltpu.SemaphoreType.DMA((half,))],
         compiler_params=pltpu.CompilerParams(vmem_limit_bytes=52 * 1024 * 1024),
-        cost_estimate=pl.CostEstimate(flops=2 * depth * tokens * blocks * cols, bytes_accessed=4_000_000, transcendentals=0),
-        name="project",
-    )(me, left, weight)
+        cost_estimate=pl.CostEstimate(flops=2 * depth * tokens * half * cols, bytes_accessed=3_000_000, transcendentals=0),
+        name=name,
+    )(side, left, weight)
 
 
 def pair_kernel(values_ref, gate_ref, out_ref, held_ref, sems):
@@ -234,8 +232,9 @@
 
     left = lax.cond(bias[0] < 1e9, there, again, left)
     me = lax.axis_index("core").astype(jnp.int32).reshape(1)
-    keep, send = project(me, left, weight)
+    send = project(1 - me, left, weight, "project_send")
     other = lax.ppermute(send, "core", [(0, 1), (1, 0)])
+    keep = project(me, left, weight, "project_keep")
     part = (keep.astype(jnp.float32) + other.astype(jnp.float32)).astype(jnp.bfloat16)
     part = part.reshape((NEAR * X,) + part.shape[2:])
     part = lax.all_to_all(part, ("zl", "y", "x"), split_axis=0, concat_axis=0, tiled=True)

time: 132 us -> 132 us (level)
    ppermute x1, waiting for transfers between devices: 1.51 us -> 0.01 us  [per_device(): other = lax.ppermute(send, 'core', [(0, 1), (1, 0)])]
    pallas_call x1 -> x2, Pallas kernels: 2.69 us -> 3.87 us  [project(): pl.pallas_call(project_kernel, out_shape=jax.ShapeDtypeStruct((tokens //...]
  transfers between devices with their start and end apart: 4 -> 4, of which waited for: 3 -> 2; matrix products, arithmetic and copies ran while one was open for 4% -> 4% of each run, Pallas kernels for 5% -> 6%
where the time goes in v5:
time: 132 us
  waiting for transfers between devices  36.7 us (28%)
  blocking collectives  35.1 us (27%)
  starting transfers between devices  30.2 us (23%)
  between operations  14.2 us (11%)
  Pallas kernels  9.55 us (7%)
  local copies, waits for them, and re-layouts  5.63 us (4%)
    all_to_all x1, blocking collectives, there(): lax.all_to_all(wide, ('zl', 'y'), split_axis=0, concat_axis=0, tiled=True)  19.4 us
    all_to_all x1, starting transfers between devices, per_device(): lax.all_to_all(both, ('zh', 'zl', 'y'), split_axis=0, concat_axis=0, tile...  19.3 us
    all_to_all x1, waiting for transfers between devices, per_device(): lax.all_to_all(both, ('zh', 'zl', 'y'), split_axis=0, concat_axis=0, tile...  19 us
    all_to_all x1, waiting for transfers between devices, per_device(): gated = lax.all_to_all(gated, 'zh', split_axis=0, concat_axis=0, tiled=True)  16.9 us
    all_to_all x1, blocking collectives, per_device(): lax.all_to_all(part, ('zl', 'y', 'x'), split_axis=0, concat_axis=0, tiled...  15.7 us
    ppermute x1, starting transfers between devices, per_device(): other = lax.ppermute(send, 'core', [(0, 1), (1, 0)])  5.64 us
    all_to_all x1, starting transfers between devices, per_device(): gated = lax.all_to_all(gated, 'zh', split_axis=0, concat_axis=0, tiled=True)  5.23 us
    pallas_call x2, Pallas kernels, project(): pl.pallas_call(project_kernel, out_shape=jax.ShapeDtypeStruct((tokens //...  3.87 us
  transfers between devices with their start and end apart: 4, of which 2 were waited for; matrix products, arithmetic and copies ran while one was open for 4% of the time, Pallas kernels for 6%

profile of v5, /device:TPU:1, one launch (start us, length us, event | category | flops | bytes accessed | tf_op | source)
XLA Modules:
  0.0 131.7 jit_solution(11054506739615591571)
XLA Ops:
  6.5 0.0 copy-start.3
  6.5 0.0 copy-start.1
  6.5 0.0 copy-start
  6.5 0.0 copy-start.2
  6.5 0.0 all-gather.3.cloned.1.call-start
  6.6 0.7 all-gather.3.cloned.1.call-update
  7.3 1.8 %pair.1 = bf16[1024,128]{1,0:T(8,128)(2,1)} custom-call(bf16[64,1024]{1,0:T(8,128)(2,1)} %values_ref.1, bf16[64,1024]{1,0:T(8,128)(2,1)} %gate_ref.1), custom_call_target="tpu_custom_call" | custom-call | tf_op jit(solution)/shard_map/pair/pallas_call | solution.py:196
  9.1 19.3 %all-to-all-start.2 = ((bf16[64,16,128]{2,1,0:T(8,128)(2,1)}), bf16[64,16,128]{2,1,0:T(8,128)(2,1)S(1)}, u32[]{:S(2)}, u32[]{:S(2)}) async-start(bf16[64,16,128]{2,1,0:T(8,128)(2,1)} %bitcast.32), calls=%async_computation.2 | async-start | bytes 524288 | tf_op jit(solution)/shard_map/all_to_all | solution.py:215
  28.4 0.8 dynamic_slice.3
  29.2 0.1 broadcast_in_dim.6
  29.2 0.1 reshape.45.skip_ref
  29.3 2.1 %reshape.44.spec_ref = f32[16,128,128]{2,1,0:T(8,128)S(1)} reshape(f32[16,2,8192]{2,1,0:T(2,128)} %param.13) | data formatting | bytes 2097152 | tf_op jit(solution)/shard_map/reshape | solution.py:219
  31.4 19.0 %all-to-all-done.2 = bf16[64,16,128]{2,1,0:T(8,128)(2,1)S(1)} async-done(((bf16[64,16,128]{2,1,0:T(8,128)(2,1)}), bf16[64,16,128]{2,1,0:T(8,128)(2,1)S(1)}, u32[]{:S(2)}, u32[]{:S(2)}) %all-to-all-start.2) | async-done | bytes 262176 | tf_op jit(solution)/shard_map/all_to_all | solution.py:215
  50.5 0.1 copy.37
  50.6 0.0 copy-done.3
  50.6 0.0 copy-done.1
  50.6 0.0 copy-done
  50.6 0.0 copy-done.2
  50.6 3.5 %gated_conv.1 = bf16[64,1024]{1,0:T(8,128)(2,1)} custom-call(bf16[16,64,128]{2,1,0:T(8,128)(2,1)S(1)} %bitcast.24, f32[16,128,128]{2,1,0:T(8,128)S(1)} %reshape.44.spec_ref, f32[1,1024]{1,0:T(1,128)S(1)} %reshape.45.skip_ref, bf16[256,128]{1,0:T(8,128)(2,1)S(1)} %copy-done.3, f32[4,128,128]{2,1,0:T(8,128)S(1)} %copy-done.1, ...), custom_call_target="tpu_custom_call" | custom-call | flops 1200000000 | bytes 2000000 | tf_op jit(solution)/shard_map/gated_conv/pallas_call | solution.py:105
  54.1 5.2 %all-to-all-start.3 = ((bf16[8,8,1024]{2,1,0:T(8,128)(2,1)}), bf16[8,8,1024]{2,1,0:T(8,128)(2,1)S(1)}, u32[]{:S(2)}, u32[]{:S(2)}) async-start(bf16[8,8,1024]{2,1,0:T(8,128)(2,1)} %bitcast.6), calls=%async_computation.3 | async-start | bytes 262144 | tf_op jit(solution)/shard_map/all_to_all | solution.py:222
  59.4 1.3 slice.3
  61.3 16.9 %all-to-all-done.3 = bf16[8,8,1024]{2,1,0:T(8,128)(2,1)S(1)} async-done(((bf16[8,8,1024]{2,1,0:T(8,128)(2,1)}), bf16[8,8,1024]{2,1,0:T(8,128)(2,1)S(1)}, u32[]{:S(2)}, u32[]{:S(2)}) %all-to-all-start.3) | async-done | bytes 131104 | tf_op jit(solution)/shard_map/all_to_all | solution.py:222
  78.2 0.2 reshape.47
  78.4 20.2 %conditional.1 = (bf16[512,1024]{1,0:T(8,128)(2,1)S(1)}) conditional(s32[]{:T(128)} %bitcast.3, bf16[8,16,8,64]{3,1,2,0:T(8,128)(2,1)S(1)} %bitcast.29, bf16[8,16,8,64]{3,1,2,0:T(8,128)(2,1)S(1)} %bitcast.30), branch_computations={%region_0.0_spmd, %region_1.0_spmd} | conditional | bytes 6815752 | solution.py:233
  78.4 0.1 copy.28
  78.5 0.2 broadcast_in_dim.0
  78.7 0.1 broadcast_in_dim.1
  78.8 19.4 %all_to_all.24.left_ref = bf16[8,8,16,512]{3,2,1,0:T(8,128)(2,1)S(1)} all-to-all(bf16[8,8,16,512]{3,2,1,0:T(8,128)(2,1)S(1)} %broadcast_in_dim.1), channel_id=1, replica_groups=mesh['zh'=8,'zl'=2,'y'=4,'x'=4,'core'=2] {'zl','y'}, dimensions={0} | all-to-all | bytes 2097152 | tf_op jit(solution)/shard_map/cond/branch_1_fun/all_to_all | solution.py:227
  98.2 0.3 turn.1
  98.6 0.0 all-gather.3.cloned.1.call-done
  98.6 1.9 %project_send.1 = bf16[8,4,64,128]{3,2,1,0:T(8,128)(2,1)S(1)} custom-call(s32[1]{0:T(128)S(6)} %sub.3.side_ref, bf16[512,1024]{1,0:T(8,128)(2,1)S(1)} %get-tuple-element.11.left_ref, bf16[8,1024,128]{2,1,0:T(8,128)(2,1)} %bitcast.25), custom_call_target="tpu_custom_call" | custom-call | flops 536870912 | bytes 3000000 | tf_op jit(solution)/shard_map/project_send/pallas_call | solution.py:172
  100.6 5.6 %collective-permute-start = (bf16[8,4,64,128]{3,2,1,0:T(8,128)(2,1)S(1)}, bf16[8,4,64,128]{3,2,1,0:T(8,128)(2,1)S(1)}, u32[]{:S(2)}, u32[]{:S(2)}) collective-permute-start(bf16[8,4,64,128]{3,2,1,0:T(8,128)(2,1)S(1)} %project_send.1), channel_id=1, source_target_pairs={{0,1},{1,0},{2,3},{3,2},{4,5},{5,4},{6,7},{7,6},{8,9},{9,8},{10,11... | collective-permute-start | bytes 1572872 | tf_op jit(solution)/shard_map/ppermute | solution.py:236
  106.2 1.9 %project_keep.1 = bf16[8,4,64,128]{3,2,1,0:T(8,128)(2,1)S(1)} custom-call(s32[1]{0:T(128)} %bitcast.2.side_ref, bf16[512,1024]{1,0:T(8,128)(2,1)S(1)} %get-tuple-element.11.left_ref, bf16[8,1024,128]{2,1,0:T(8,128)(2,1)} %bitcast.26), custom_call_target="tpu_custom_call" | custom-call | flops 536870912 | bytes 3000000 | tf_op jit(solution)/shard_map/project_keep/pallas_call | solution.py:172
  108.2 0.0 collective-permute-done
  108.2 0.2 add_convert_fusion
  108.4 15.7 %all_to_all.25 = bf16[32,64,128]{2,1,0:T(8,128)(2,1)S(1)} all-to-all(bf16[32,64,128]{2,1,0:T(8,128)(2,1)S(1)} %bitcast.31), channel_id=1, replica_groups=mesh['zh'=8,'zl'=2,'y'=4,'x'=4,'core'=2] {'zl','y','x'}, dimensions={0} | all-to-all | bytes 1048576 | tf_op jit(solution)/shard_map/all_to_all | solution.py:240
  124.1 0.1 bitcast_reduce_fusion
  124.2 0.7 copy_bitcast_fusion.1
Async XLA Ops:
  6.5 44.0 %copy-start.3 = (bf16[256,128]{1,0:T(8,128)(2,1)S(1)}, bf16[256,128]{1,0:T(8,128)(2,1)}, u32[]{:S(2)}) copy-start(bf16[256,128]{1,0:T(8,128)(2,1)} %constant.44.clone.first_ref) | copy-start | bytes 196612
  6.5 44.0 %copy-start.1 = (f32[4,128,128]{2,1,0:T(8,128)S(1)}, f32[4,128,128]{2,1,0:T(8,128)}, u32[]{:S(2)}) copy-start(f32[4,128,128]{2,1,0:T(8,128)} %constant.45.clone.spin_ref) | copy-start | bytes 786436
  6.5 44.0 %copy-start = (bf16[2,384,256]{2,1,0:T(8,128)(2,1)S(1)}, bf16[2,384,256]{2,1,0:T(8,128)(2,1)}, u32[]{:S(2)}) copy-start(bf16[2,384,256]{2,1,0:T(8,128)(2,1)} %constant.46.clone.mid_ref) | copy-start | bytes 1179652
  6.5 44.0 %copy-start.2 = (bf16[128,384]{1,0:T(8,128)(2,1)S(1)}, bf16[128,384]{1,0:T(8,128)(2,1)}, u32[]{:S(2)}) copy-start(bf16[128,384]{1,0:T(8,128)(2,1)} %constant.47.clone.last_ref) | copy-start | bytes 294916
  6.5 92.1 %all-gather.3.cloned.1.call-start = ((), (), s32[]{:S(2)}) async-start(), calls=%async_computation.5 | async-start | bytes 2359296 | tf_op jit(solution)/shard_map/all_gather | solution.py:211
  9.1 41.4 %all-to-all-start.2 = ((bf16[64,16,128]{2,1,0:T(8,128)(2,1)}), bf16[64,16,128]{2,1,0:T(8,128)(2,1)S(1)}, u32[]{:S(2)}, u32[]{:S(2)}) async-start(bf16[64,16,128]{2,1,0:T(8,128)(2,1)} %bitcast.32), calls=%async_computation.2 | async-start | bytes 524288 | tf_op jit(solution)/shard_map/all_to_all | solution.py:215
  54.1 24.1 %all-to-all-start.3 = ((bf16[8,8,1024]{2,1,0:T(8,128)(2,1)}), bf16[8,8,1024]{2,1,0:T(8,128)(2,1)S(1)}, u32[]{:S(2)}, u32[]{:S(2)}) async-start(bf16[8,8,1024]{2,1,0:T(8,128)(2,1)} %bitcast.6), calls=%async_computation.3 | async-start | bytes 262144 | tf_op jit(solution)/shard_map/all_to_all | solution.py:222
  100.6 7.6 %collective-permute-start = (bf16[8,4,64,128]{3,2,1,0:T(8,128)(2,1)S(1)}, bf16[8,4,64,128]{3,2,1,0:T(8,128)(2,1)S(1)}, u32[]{:S(2)}, u32[]{:S(2)}) collective-permute-start(bf16[8,4,64,128]{3,2,1,0:T(8,128)(2,1)S(1)} %project_send.1), channel_id=1, source_target_pairs={{0,1},{1,0},{2,3},{3,2},{4,5},{5,4},{6,7},{7,6},{8,9},{9,8},{10,11... | collective-permute-start | bytes 1572872 | tf_op jit(solution)/shard_map/ppermute | solution.py:236
Sparse Core Ops, SparseCore 0:
  9.5 84.5 all-gather.2

commit v6 on v5

--- a/solution.py
+++ b/solution.py
@@ -56,7 +56,7 @@
     return [top, rest, top]
 
 
-GANG = 8
+GANG = 16
 
 
 def conv_kernel(both_ref, spec_ref, skip_ref, first_ref, spin_ref, mid_ref, last_ref, out_ref):

time: 132 us -> 132 us (level)
  no operation moved by 1% of the time
where the time goes in v6:
time: 132 us
  waiting for transfers between devices  36.8 us (28%)
  blocking collectives  35.1 us (27%)
  starting transfers between devices  30.3 us (23%)
  between operations  14.2 us (11%)
  Pallas kernels  9.3 us (7%)
  local copies, waits for them, and re-layouts  5.63 us (4%)
    all_to_all x1, blocking collectives, there(): lax.all_to_all(wide, ('zl', 'y'), split_axis=0, concat_axis=0, tiled=True)  19.5 us
    all_to_all x1, starting transfers between devices, per_device(): lax.all_to_all(both, ('zh', 'zl', 'y'), split_axis=0, concat_axis=0, tile...  19.3 us
    all_to_all x1, waiting for transfers between devices, per_device(): lax.all_to_all(both, ('zh', 'zl', 'y'), split_axis=0, concat_axis=0, tile...  19 us
    all_to_all x1, waiting for transfers between devices, per_device(): gated = lax.all_to_all(gated, 'zh', split_axis=0, concat_axis=0, tiled=True)  17.1 us
    all_to_all x1, blocking collectives, per_device(): lax.all_to_all(part, ('zl', 'y', 'x'), split_axis=0, concat_axis=0, tiled...  15.5 us
    ppermute x1, starting transfers between devices, per_device(): other = lax.ppermute(send, 'core', [(0, 1), (1, 0)])  5.75 us
    all_to_all x1, starting transfers between devices, per_device(): gated = lax.all_to_all(gated, 'zh', split_axis=0, concat_axis=0, tiled=True)  5.23 us
    pallas_call x2, Pallas kernels, project(): pl.pallas_call(project_kernel, out_shape=jax.ShapeDtypeStruct((tokens //...  3.87 us
  transfers between devices with their start and end apart: 4, of which 2 were waited for; matrix products, arithmetic and copies ran while one was open for 4% of the time, Pallas kernels for 6%

profile of v6, /device:TPU:1, one launch (start us, length us, event | category | flops | bytes accessed | tf_op | source)
XLA Modules:
  0.0 131.6 jit_solution(12767534053022612549)
XLA Ops:
  6.5 0.0 copy-start.3
  6.5 0.0 copy-start.1
  6.5 0.0 copy-start
  6.5 0.0 copy-start.2
  6.5 0.0 all-gather.3.cloned.1.call-start
  6.6 0.7 all-gather.3.cloned.1.call-update
  7.3 1.8 %pair.1 = bf16[1024,128]{1,0:T(8,128)(2,1)} custom-call(bf16[64,1024]{1,0:T(8,128)(2,1)} %values_ref.1, bf16[64,1024]{1,0:T(8,128)(2,1)} %gate_ref.1), custom_call_target="tpu_custom_call" | custom-call | tf_op jit(solution)/shard_map/pair/pallas_call | solution.py:196
  9.1 19.3 %all-to-all-start.2 = ((bf16[64,16,128]{2,1,0:T(8,128)(2,1)}), bf16[64,16,128]{2,1,0:T(8,128)(2,1)S(1)}, u32[]{:S(2)}, u32[]{:S(2)}) async-start(bf16[64,16,128]{2,1,0:T(8,128)(2,1)} %bitcast.32), calls=%async_computation.2 | async-start | bytes 524288 | tf_op jit(solution)/shard_map/all_to_all | solution.py:215
  28.4 0.8 dynamic_slice.3
  29.2 0.1 broadcast_in_dim.6
  29.2 0.1 reshape.45.skip_ref
  29.3 2.1 %reshape.44.spec_ref = f32[16,128,128]{2,1,0:T(8,128)S(1)} reshape(f32[16,2,8192]{2,1,0:T(2,128)} %param.13) | data formatting | bytes 2097152 | tf_op jit(solution)/shard_map/reshape | solution.py:219
  31.4 19.0 %all-to-all-done.2 = bf16[64,16,128]{2,1,0:T(8,128)(2,1)S(1)} async-done(((bf16[64,16,128]{2,1,0:T(8,128)(2,1)}), bf16[64,16,128]{2,1,0:T(8,128)(2,1)S(1)}, u32[]{:S(2)}, u32[]{:S(2)}) %all-to-all-start.2) | async-done | bytes 262176 | tf_op jit(solution)/shard_map/all_to_all | solution.py:215
  50.5 0.1 copy.37
  50.6 0.0 copy-done.3
  50.6 0.0 copy-done.1
  50.6 0.0 copy-done
  50.6 0.0 copy-done.2
  50.6 3.3 %gated_conv.1 = bf16[64,1024]{1,0:T(8,128)(2,1)} custom-call(bf16[16,64,128]{2,1,0:T(8,128)(2,1)S(1)} %bitcast.24, f32[16,128,128]{2,1,0:T(8,128)S(1)} %reshape.44.spec_ref, f32[1,1024]{1,0:T(1,128)S(1)} %reshape.45.skip_ref, bf16[256,128]{1,0:T(8,128)(2,1)S(1)} %copy-done.3, f32[4,128,128]{2,1,0:T(8,128)S(1)} %copy-done.1, ...), custom_call_target="tpu_custom_call" | custom-call | flops 1200000000 | bytes 2000000 | tf_op jit(solution)/shard_map/gated_conv/pallas_call | solution.py:105
  53.9 5.2 %all-to-all-start.3 = ((bf16[8,8,1024]{2,1,0:T(8,128)(2,1)}), bf16[8,8,1024]{2,1,0:T(8,128)(2,1)S(1)}, u32[]{:S(2)}, u32[]{:S(2)}) async-start(bf16[8,8,1024]{2,1,0:T(8,128)(2,1)} %bitcast.6), calls=%async_computation.3 | async-start | bytes 262144 | tf_op jit(solution)/shard_map/all_to_all | solution.py:222
  59.1 1.3 slice.3
  61.1 17.1 %all-to-all-done.3 = bf16[8,8,1024]{2,1,0:T(8,128)(2,1)S(1)} async-done(((bf16[8,8,1024]{2,1,0:T(8,128)(2,1)}), bf16[8,8,1024]{2,1,0:T(8,128)(2,1)S(1)}, u32[]{:S(2)}, u32[]{:S(2)}) %all-to-all-start.3) | async-done | bytes 131104 | tf_op jit(solution)/shard_map/all_to_all | solution.py:222
  78.1 0.2 reshape.47
  78.3 20.3 %conditional.1 = (bf16[512,1024]{1,0:T(8,128)(2,1)S(1)}) conditional(s32[]{:T(128)} %bitcast.3, bf16[8,16,8,64]{3,1,2,0:T(8,128)(2,1)S(1)} %bitcast.29, bf16[8,16,8,64]{3,1,2,0:T(8,128)(2,1)S(1)} %bitcast.30), branch_computations={%region_0.0_spmd, %region_1.0_spmd} | conditional | bytes 6815752 | solution.py:233
  78.3 0.1 copy.28
  78.4 0.2 broadcast_in_dim.0
  78.6 0.1 broadcast_in_dim.1
  78.8 19.5 %all_to_all.24.left_ref = bf16[8,8,16,512]{3,2,1,0:T(8,128)(2,1)S(1)} all-to-all(bf16[8,8,16,512]{3,2,1,0:T(8,128)(2,1)S(1)} %broadcast_in_dim.1), channel_id=1, replica_groups=mesh['zh'=8,'zl'=2,'y'=4,'x'=4,'core'=2] {'zl','y'}, dimensions={0} | all-to-all | bytes 2097152 | tf_op jit(solution)/shard_map/cond/branch_1_fun/all_to_all | solution.py:227
  98.3 0.3 turn.1
  98.6 0.0 all-gather.3.cloned.1.call-done
  98.7 1.9 %project_send.1 = bf16[8,4,64,128]{3,2,1,0:T(8,128)(2,1)S(1)} custom-call(s32[1]{0:T(128)S(6)} %sub.3.side_ref, bf16[512,1024]{1,0:T(8,128)(2,1)S(1)} %get-tuple-element.11.left_ref, bf16[8,1024,128]{2,1,0:T(8,128)(2,1)} %bitcast.25), custom_call_target="tpu_custom_call" | custom-call | flops 536870912 | bytes 3000000 | tf_op jit(solution)/shard_map/project_send/pallas_call | solution.py:172
  100.6 5.8 %collective-permute-start = (bf16[8,4,64,128]{3,2,1,0:T(8,128)(2,1)S(1)}, bf16[8,4,64,128]{3,2,1,0:T(8,128)(2,1)S(1)}, u32[]{:S(2)}, u32[]{:S(2)}) collective-permute-start(bf16[8,4,64,128]{3,2,1,0:T(8,128)(2,1)S(1)} %project_send.1), channel_id=1, source_target_pairs={{0,1},{1,0},{2,3},{3,2},{4,5},{5,4},{6,7},{7,6},{8,9},{9,8},{10,11... | collective-permute-start | bytes 1572872 | tf_op jit(solution)/shard_map/ppermute | solution.py:236
  106.4 1.9 %project_keep.1 = bf16[8,4,64,128]{3,2,1,0:T(8,128)(2,1)S(1)} custom-call(s32[1]{0:T(128)} %bitcast.2.side_ref, bf16[512,1024]{1,0:T(8,128)(2,1)S(1)} %get-tuple-element.11.left_ref, bf16[8,1024,128]{2,1,0:T(8,128)(2,1)} %bitcast.26), custom_call_target="tpu_custom_call" | custom-call | flops 536870912 | bytes 3000000 | tf_op jit(solution)/shard_map/project_keep/pallas_call | solution.py:172
  108.3 0.0 collective-permute-done
  108.3 0.2 add_convert_fusion
  108.5 15.5 %all_to_all.25 = bf16[32,64,128]{2,1,0:T(8,128)(2,1)S(1)} all-to-all(bf16[32,64,128]{2,1,0:T(8,128)(2,1)S(1)} %bitcast.31), channel_id=1, replica_groups=mesh['zh'=8,'zl'=2,'y'=4,'x'=4,'core'=2] {'zl','y','x'}, dimensions={0} | all-to-all | bytes 1048576 | tf_op jit(solution)/shard_map/all_to_all | solution.py:240
  124.0 0.1 bitcast_reduce_fusion
  124.1 0.7 copy_bitcast_fusion.1
Async XLA Ops:
  6.5 44.0 %copy-start.3 = (bf16[256,128]{1,0:T(8,128)(2,1)S(1)}, bf16[256,128]{1,0:T(8,128)(2,1)}, u32[]{:S(2)}) copy-start(bf16[256,128]{1,0:T(8,128)(2,1)} %constant.44.clone.first_ref) | copy-start | bytes 196612
  6.5 44.0 %copy-start.1 = (f32[4,128,128]{2,1,0:T(8,128)S(1)}, f32[4,128,128]{2,1,0:T(8,128)}, u32[]{:S(2)}) copy-start(f32[4,128,128]{2,1,0:T(8,128)} %constant.45.clone.spin_ref) | copy-start | bytes 786436
  6.5 44.0 %copy-start = (bf16[2,384,256]{2,1,0:T(8,128)(2,1)S(1)}, bf16[2,384,256]{2,1,0:T(8,128)(2,1)}, u32[]{:S(2)}) copy-start(bf16[2,384,256]{2,1,0:T(8,128)(2,1)} %constant.46.clone.mid_ref) | copy-start | bytes 1179652
  6.5 44.0 %copy-start.2 = (bf16[128,384]{1,0:T(8,128)(2,1)S(1)}, bf16[128,384]{1,0:T(8,128)(2,1)}, u32[]{:S(2)}) copy-start(bf16[128,384]{1,0:T(8,128)(2,1)} %constant.47.clone.last_ref) | copy-start | bytes 294916
  6.5 92.1 %all-gather.3.cloned.1.call-start = ((), (), s32[]{:S(2)}) async-start(), calls=%async_computation.5 | async-start | bytes 2359296 | tf_op jit(solution)/shard_map/all_gather | solution.py:211
  9.1 41.4 %all-to-all-start.2 = ((bf16[64,16,128]{2,1,0:T(8,128)(2,1)}), bf16[64,16,128]{2,1,0:T(8,128)(2,1)S(1)}, u32[]{:S(2)}, u32[]{:S(2)}) async-start(bf16[64,16,128]{2,1,0:T(8,128)(2,1)} %bitcast.32), calls=%async_computation.2 | async-start | bytes 524288 | tf_op jit(solution)/shard_map/all_to_all | solution.py:215
  53.9 24.3 %all-to-all-start.3 = ((bf16[8,8,1024]{2,1,0:T(8,128)(2,1)}), bf16[8,8,1024]{2,1,0:T(8,128)(2,1)S(1)}, u32[]{:S(2)}, u32[]{:S(2)}) async-start(bf16[8,8,1024]{2,1,0:T(8,128)(2,1)} %bitcast.6), calls=%async_computation.3 | async-start | bytes 262144 | tf_op jit(solution)/shard_map/all_to_all | solution.py:222
  100.6 7.7 %collective-permute-start = (bf16[8,4,64,128]{3,2,1,0:T(8,128)(2,1)S(1)}, bf16[8,4,64,128]{3,2,1,0:T(8,128)(2,1)S(1)}, u32[]{:S(2)}, u32[]{:S(2)}) collective-permute-start(bf16[8,4,64,128]{3,2,1,0:T(8,128)(2,1)S(1)} %project_send.1), channel_id=1, source_target_pairs={{0,1},{1,0},{2,3},{3,2},{4,5},{5,4},{6,7},{7,6},{8,9},{9,8},{10,11... | collective-permute-start | bytes 1572872 | tf_op jit(solution)/shard_map/ppermute | solution.py:236
Sparse Core Ops, SparseCore 0:
  9.5 84.8 all-gather.2

commit v7 on v6

--- a/solution.py
+++ b/solution.py
@@ -181,13 +181,32 @@
     )(side, left, weight)
 
 
-def pair_kernel(values_ref, gate_ref, out_ref, held_ref, sems):
-    copies = [pltpu.make_async_copy(ref, held_ref.at[i], sems.at[i]) for i, ref in enumerate((values_ref, gate_ref))]
-    for copy in copies:
-        copy.start()
-    for copy in copies:
+PARTS = 2
+
+
+def pair_kernel(values_ref, gate_ref, out_ref, held_ref, turned_ref, sems):
+    wide = values_ref.shape[1] // PARTS
+    at = [pl.ds(part * wide, wide) for part in range(PARTS)]
+    arrive = [
+        [
+            pltpu.make_async_copy(ref.at[:, at[part]], held_ref.at[part, i], sems.at[part * 3 + i])
+            for i, ref in enumerate((values_ref, gate_ref))
+        ]
+        for part in range(PARTS)
+    ]
+    leave = [
+        pltpu.make_async_copy(turned_ref.at[part], out_ref.at[at[part]], sems.at[part * 3 + 2]) for part in range(PARTS)
+    ]
+    for copies in arrive:
+        for copy in copies:
+            copy.start()
+    for part in range(PARTS):
+        for copy in arrive[part]:
+            copy.wait()
+        turned_ref[part] = jnp.concatenate([held_ref[part, 0], held_ref[part, 1]], 0).T
+        leave[part].start()
+    for copy in leave:
         copy.wait()
-    out_ref[...] = jnp.concatenate([held_ref[0], held_ref[1]], 0).T
 
 
 def pair(values, gate):
@@ -197,8 +216,12 @@
         pair_kernel,
         out_shape=jax.ShapeDtypeStruct((group, 2 * rows), jnp.bfloat16),
         in_specs=[away, away],
-        out_specs=pl.BlockSpec(memory_space=pltpu.VMEM),
-        scratch_shapes=[pltpu.VMEM((2, rows, group), jnp.bfloat16), pltpu.SemaphoreType.DMA((2,))],
+        out_specs=away,
+        scratch_shapes=[
+            pltpu.VMEM((PARTS, 2, rows, group // PARTS), jnp.bfloat16),
+            pltpu.VMEM((PARTS, group // PARTS, 2 * rows), jnp.bfloat16),
+            pltpu.SemaphoreType.DMA((3 * PARTS,)),
+        ],
         compiler_params=pltpu.CompilerParams(vmem_limit_bytes=56 * 1024 * 1024),
         name="pair",
     )(values, gate)

time: 132 us -> 132 us (level)
  no operation moved by 1% of the time
where the time goes in v7:
time: 132 us; the launch traced here: 131 us
  waiting for transfers between devices  36.8 us (28%)
  blocking collectives  34.9 us (26%)
  starting transfers between devices  30.3 us (23%)
  between operations  14.2 us (11%)
  Pallas kernels  9.25 us (7%)
  local copies, waits for them, and re-layouts  5.63 us (4%)
    all_to_all x1, blocking collectives, there(): lax.all_to_all(wide, ('zl', 'y'), split_axis=0, concat_axis=0, tiled=True)  19.6 us
    all_to_all x1, starting transfers between devices, per_device(): lax.all_to_all(both, ('zh', 'zl', 'y'), split_axis=0, concat_axis=0, tile...  19.3 us
    all_to_all x1, waiting for transfers between devices, per_device(): lax.all_to_all(both, ('zh', 'zl', 'y'), split_axis=0, concat_axis=0, tile...  19.1 us
    all_to_all x1, waiting for transfers between devices, per_device(): gated = lax.all_to_all(gated, 'zh', split_axis=0, concat_axis=0, tiled=True)  17.1 us
    all_to_all x1, blocking collectives, per_device(): lax.all_to_all(part, ('zl', 'y', 'x'), split_axis=0, concat_axis=0, tiled...  15.3 us
    ppermute x1, starting transfers between devices, per_device(): other = lax.ppermute(send, 'core', [(0, 1), (1, 0)])  5.78 us
    all_to_all x1, starting transfers between devices, per_device(): gated = lax.all_to_all(gated, 'zh', split_axis=0, concat_axis=0, tiled=True)  5.2 us
    pallas_call x2, Pallas kernels, project(): pl.pallas_call(project_kernel, out_shape=jax.ShapeDtypeStruct((tokens //...  3.87 us
  transfers between devices with their start and end apart: 4, of which 2 were waited for; matrix products, arithmetic and copies ran while one was open for 4% of the time, Pallas kernels for 6%

profile of v7, /device:TPU:1, one launch (start us, length us, event | category | flops | bytes accessed | tf_op | source)
XLA Modules:
  0.0 131.4 jit_solution(7671989164741279745)
XLA Ops:
  6.5 0.0 copy-start.3
  6.5 0.0 copy-start.1
  6.5 0.0 copy-start
  6.5 0.0 copy-start.2
  6.5 0.0 all-gather.3.cloned.1.call-start
  6.6 0.7 all-gather.3.cloned.1.call-update
  7.3 1.8 %pair.1 = bf16[1024,128]{1,0:T(8,128)(2,1)} custom-call(bf16[64,1024]{1,0:T(8,128)(2,1)} %values_ref.1, bf16[64,1024]{1,0:T(8,128)(2,1)} %gate_ref.1), custom_call_target="tpu_custom_call" | custom-call | tf_op jit(solution)/shard_map/pair/pallas_call | solution.py:215
  9.0 19.3 %all-to-all-start.2 = ((bf16[64,16,128]{2,1,0:T(8,128)(2,1)}), bf16[64,16,128]{2,1,0:T(8,128)(2,1)S(1)}, u32[]{:S(2)}, u32[]{:S(2)}) async-start(bf16[64,16,128]{2,1,0:T(8,128)(2,1)} %bitcast.32), calls=%async_computation.2 | async-start | bytes 524288 | tf_op jit(solution)/shard_map/all_to_all | solution.py:238
  28.3 0.8 dynamic_slice.3
  29.1 0.1 broadcast_in_dim.6
  29.2 0.1 reshape.45.skip_ref
  29.3 2.1 %reshape.44.spec_ref = f32[16,128,128]{2,1,0:T(8,128)S(1)} reshape(f32[16,2,8192]{2,1,0:T(2,128)} %param.13) | data formatting | bytes 2097152 | tf_op jit(solution)/shard_map/reshape | solution.py:242
  31.4 19.1 %all-to-all-done.2 = bf16[64,16,128]{2,1,0:T(8,128)(2,1)S(1)} async-done(((bf16[64,16,128]{2,1,0:T(8,128)(2,1)}), bf16[64,16,128]{2,1,0:T(8,128)(2,1)S(1)}, u32[]{:S(2)}, u32[]{:S(2)}) %all-to-all-start.2) | async-done | bytes 262176 | tf_op jit(solution)/shard_map/all_to_all | solution.py:238
  50.5 0.1 copy.37
  50.5 0.0 copy-done.3
  50.5 0.0 copy-done.1
  50.5 0.0 copy-done
  50.6 0.0 copy-done.2
  50.6 3.3 %gated_conv.1 = bf16[64,1024]{1,0:T(8,128)(2,1)} custom-call(bf16[16,64,128]{2,1,0:T(8,128)(2,1)S(1)} %bitcast.24, f32[16,128,128]{2,1,0:T(8,128)S(1)} %reshape.44.spec_ref, f32[1,1024]{1,0:T(1,128)S(1)} %reshape.45.skip_ref, bf16[256,128]{1,0:T(8,128)(2,1)S(1)} %copy-done.3, f32[4,128,128]{2,1,0:T(8,128)S(1)} %copy-done.1, ...), custom_call_target="tpu_custom_call" | custom-call | flops 1200000000 | bytes 2000000 | tf_op jit(solution)/shard_map/gated_conv/pallas_call | solution.py:105
  53.9 5.2 %all-to-all-start.3 = ((bf16[8,8,1024]{2,1,0:T(8,128)(2,1)}), bf16[8,8,1024]{2,1,0:T(8,128)(2,1)S(1)}, u32[]{:S(2)}, u32[]{:S(2)}) async-start(bf16[8,8,1024]{2,1,0:T(8,128)(2,1)} %bitcast.6), calls=%async_computation.3 | async-start | bytes 262144 | tf_op jit(solution)/shard_map/all_to_all | solution.py:245
  59.1 1.3 slice.3
  61.0 17.1 %all-to-all-done.3 = bf16[8,8,1024]{2,1,0:T(8,128)(2,1)S(1)} async-done(((bf16[8,8,1024]{2,1,0:T(8,128)(2,1)}), bf16[8,8,1024]{2,1,0:T(8,128)(2,1)S(1)}, u32[]{:S(2)}, u32[]{:S(2)}) %all-to-all-start.3) | async-done | bytes 131104 | tf_op jit(solution)/shard_map/all_to_all | solution.py:245
  78.0 0.2 reshape.47
  78.2 20.4 %conditional.1 = (bf16[512,1024]{1,0:T(8,128)(2,1)S(1)}) conditional(s32[]{:T(128)} %bitcast.3, bf16[8,16,8,64]{3,1,2,0:T(8,128)(2,1)S(1)} %bitcast.29, bf16[8,16,8,64]{3,1,2,0:T(8,128)(2,1)S(1)} %bitcast.30), branch_computations={%region_0.0_spmd, %region_1.0_spmd} | conditional | bytes 6815752 | solution.py:256
  78.3 0.1 copy.28
  78.3 0.2 broadcast_in_dim.0
  78.5 0.1 broadcast_in_dim.1
  78.7 19.6 %all_to_all.24.left_ref = bf16[8,8,16,512]{3,2,1,0:T(8,128)(2,1)S(1)} all-to-all(bf16[8,8,16,512]{3,2,1,0:T(8,128)(2,1)S(1)} %broadcast_in_dim.1), channel_id=1, replica_groups=mesh['zh'=8,'zl'=2,'y'=4,'x'=4,'core'=2] {'zl','y'}, dimensions={0} | all-to-all | bytes 2097152 | tf_op jit(solution)/shard_map/cond/branch_1_fun/all_to_all | solution.py:250
  98.3 0.3 turn.1
  98.6 0.0 all-gather.3.cloned.1.call-done
  98.6 1.9 %project_send.1 = bf16[8,4,64,128]{3,2,1,0:T(8,128)(2,1)S(1)} custom-call(s32[1]{0:T(128)S(6)} %sub.3.side_ref, bf16[512,1024]{1,0:T(8,128)(2,1)S(1)} %get-tuple-element.11.left_ref, bf16[8,1024,128]{2,1,0:T(8,128)(2,1)} %bitcast.25), custom_call_target="tpu_custom_call" | custom-call | flops 536870912 | bytes 3000000 | tf_op jit(solution)/shard_map/project_send/pallas_call | solution.py:172
  100.6 5.8 %collective-permute-start = (bf16[8,4,64,128]{3,2,1,0:T(8,128)(2,1)S(1)}, bf16[8,4,64,128]{3,2,1,0:T(8,128)(2,1)S(1)}, u32[]{:S(2)}, u32[]{:S(2)}) collective-permute-start(bf16[8,4,64,128]{3,2,1,0:T(8,128)(2,1)S(1)} %project_send.1), channel_id=1, source_target_pairs={{0,1},{1,0},{2,3},{3,2},{4,5},{5,4},{6,7},{7,6},{8,9},{9,8},{10,11... | collective-permute-start | bytes 1572872 | tf_op jit(solution)/shard_map/ppermute | solution.py:259
  106.4 1.9 %project_keep.1 = bf16[8,4,64,128]{3,2,1,0:T(8,128)(2,1)S(1)} custom-call(s32[1]{0:T(128)} %bitcast.2.side_ref, bf16[512,1024]{1,0:T(8,128)(2,1)S(1)} %get-tuple-element.11.left_ref, bf16[8,1024,128]{2,1,0:T(8,128)(2,1)} %bitcast.26), custom_call_target="tpu_custom_call" | custom-call | flops 536870912 | bytes 3000000 | tf_op jit(solution)/shard_map/project_keep/pallas_call | solution.py:172
  108.3 0.0 collective-permute-done
  108.3 0.2 add_convert_fusion
  108.5 15.3 %all_to_all.25 = bf16[32,64,128]{2,1,0:T(8,128)(2,1)S(1)} all-to-all(bf16[32,64,128]{2,1,0:T(8,128)(2,1)S(1)} %bitcast.31), channel_id=1, replica_groups=mesh['zh'=8,'zl'=2,'y'=4,'x'=4,'core'=2] {'zl','y','x'}, dimensions={0} | all-to-all | bytes 1048576 | tf_op jit(solution)/shard_map/all_to_all | solution.py:263
  123.8 0.1 bitcast_reduce_fusion
  123.9 0.7 copy_bitcast_fusion.1
Async XLA Ops:
  6.5 44.0 %copy-start.3 = (bf16[256,128]{1,0:T(8,128)(2,1)S(1)}, bf16[256,128]{1,0:T(8,128)(2,1)}, u32[]{:S(2)}) copy-start(bf16[256,128]{1,0:T(8,128)(2,1)} %constant.44.clone.first_ref) | copy-start | bytes 196612
  6.5 44.0 %copy-start.1 = (f32[4,128,128]{2,1,0:T(8,128)S(1)}, f32[4,128,128]{2,1,0:T(8,128)}, u32[]{:S(2)}) copy-start(f32[4,128,128]{2,1,0:T(8,128)} %constant.45.clone.spin_ref) | copy-start | bytes 786436
  6.5 44.0 %copy-start = (bf16[2,384,256]{2,1,0:T(8,128)(2,1)S(1)}, bf16[2,384,256]{2,1,0:T(8,128)(2,1)}, u32[]{:S(2)}) copy-start(bf16[2,384,256]{2,1,0:T(8,128)(2,1)} %constant.46.clone.mid_ref) | copy-start | bytes 1179652
  6.5 44.0 %copy-start.2 = (bf16[128,384]{1,0:T(8,128)(2,1)S(1)}, bf16[128,384]{1,0:T(8,128)(2,1)}, u32[]{:S(2)}) copy-start(bf16[128,384]{1,0:T(8,128)(2,1)} %constant.47.clone.last_ref) | copy-start | bytes 294916
  6.5 92.1 %all-gather.3.cloned.1.call-start = ((), (), s32[]{:S(2)}) async-start(), calls=%async_computation.5 | async-start | bytes 2359296 | tf_op jit(solution)/shard_map/all_gather | solution.py:234
  9.0 41.4 %all-to-all-start.2 = ((bf16[64,16,128]{2,1,0:T(8,128)(2,1)}), bf16[64,16,128]{2,1,0:T(8,128)(2,1)S(1)}, u32[]{:S(2)}, u32[]{:S(2)}) async-start(bf16[64,16,128]{2,1,0:T(8,128)(2,1)} %bitcast.32), calls=%async_computation.2 | async-start | bytes 524288 | tf_op jit(solution)/shard_map/all_to_all | solution.py:238
  53.9 24.2 %all-to-all-start.3 = ((bf16[8,8,1024]{2,1,0:T(8,128)(2,1)}), bf16[8,8,1024]{2,1,0:T(8,128)(2,1)S(1)}, u32[]{:S(2)}, u32[]{:S(2)}) async-start(bf16[8,8,1024]{2,1,0:T(8,128)(2,1)} %bitcast.6), calls=%async_computation.3 | async-start | bytes 262144 | tf_op jit(solution)/shard_map/all_to_all | solution.py:245
  100.6 7.7 %collective-permute-start = (bf16[8,4,64,128]{3,2,1,0:T(8,128)(2,1)S(1)}, bf16[8,4,64,128]{3,2,1,0:T(8,128)(2,1)S(1)}, u32[]{:S(2)}, u32[]{:S(2)}) collective-permute-start(bf16[8,4,64,128]{3,2,1,0:T(8,128)(2,1)S(1)} %project_send.1), channel_id=1, source_target_pairs={{0,1},{1,0},{2,3},{3,2},{4,5},{5,4},{6,7},{7,6},{8,9},{9,8},{10,11... | collective-permute-start | bytes 1572872 | tf_op jit(solution)/shard_map/ppermute | solution.py:259
Sparse Core Ops, SparseCore 0:
  9.5 84.5 all-gather.2
